TPU v7x, 256 devices: a whole 4x4x8 slice. The times are simulated.
256 devices in a mesh: fibre: 16 (over z, core), rest: 16 (over x, y).
Axes of the slice: x: 4, y: 4, z: 8, core: 2. Of those that a mesh axis runs over, the one named last changes fastest.
Arguments:
- slab: float32 [672, 262144], P('fibre', 'rest'), may hold values from -6 to 6
- start_basis: float32 [672, 96], replicated, may hold values from -6 to 6
Outputs:
- factor: float32 [672, 96], replicated
- core: float32 [96, 262144], P('fibre', 'rest')
All inputs are finite; a program needn't handle non-finite values.
Results may differ from a plain program's by a relative error of at most 0.00023.
Values sent between devices are 32-bit elements; how exact they have to be, the bound alone decides.
A program may use at most 64 MiB of HBM per device.

v0:
```python
import jax
import jax.numpy as jnp
from jax import lax
from jax.sharding import PartitionSpec as P

ITERS = 3


def orthonormal(image, small):
    lower = jnp.linalg.cholesky(small)
    return lax.linalg.triangular_solve(lower, image, left_side=False, lower=True, transpose_a=True)


def shards(slab, start_basis):
    hp = lax.Precision.HIGHEST
    fibres = lax.all_to_all(slab, "fibre", split_axis=1, concat_axis=0, tiled=True)
    partial_gram = jnp.dot(fibres, fibres.T, precision=hp, preferred_element_type=jnp.float32)
    own_rows = slab.shape[0]
    first_row = lax.axis_index("fibre") * own_rows
    basis = start_basis
    gram = lax.psum(partial_gram, ("fibre", "rest"))
    for step in range(ITERS):
        image = jnp.dot(gram, basis, precision=hp, preferred_element_type=jnp.float32)
        small = jnp.dot(image.T, image, precision=hp, preferred_element_type=jnp.float32)
        basis = orthonormal(image, small)
    own_basis = lax.dynamic_slice_in_dim(basis, first_row, own_rows, 0)
    core = lax.psum_scatter(
        jnp.dot(own_basis.T, slab, precision=hp, preferred_element_type=jnp.float32),
        "fibre",
        scatter_dimension=0,
        tiled=True,
    )
    return (basis, core)


def solution(mesh):
    return jax.shard_map(
        shards,
        mesh=mesh,
        in_specs=(P("fibre", "rest"), P()),
        out_specs=(P(), P("fibre", "rest")),
        check_vma=False,
    )
```

profile of v0, /device:TPU:163, one launch (start us, length us, event | category | flops | bytes accessed | tf_op | source)
XLA Modules:
  0.0 572.0 jit_solution(11799792493297512326)
XLA Ops:
  7.2 3.7 copy.15
  11.3 1.6 copy.11
  12.9 76.3 %all_to_all.19 = f32[42,16,1024]{2,0,1:T(8,128)} all-to-all(f32[42,16,1024]{2,0,1:T(8,128)S(1)} %copy.11), channel_id=1, replica_groups=mesh['fibre'=16,'rest'=16] {'fibre'}, dimensions={1} | all-to-all | bytes 5505024 | tf_op jit(solution)/shard_map/all_to_all | solution.py:16
  89.3 2.2 all_to_all.17
  91.5 8.0 %fusion.17 = f32[672,672]{1,0:T(8,128)} fusion(f32[672,1024]{1,0:T(8,128)S(1)} %all_to_all.17), kind=kOutput, calls=%fused_computation.32 | convolution fusion | flops 5549064192 | bytes 4558848 | tf_op jit(solution)/shard_map/dot_general | solution.py:17
  99.6 259.0 %all-reduce.4.cloned.1.call-done = f32[672,672]{1,0:T(8,128)} async-done(((f32[672,672]{1,0:T(8,128)}), f32[672,672]{1,0:T(8,128)}) %all-reduce.4.cloned.1.call-update) | async-done | bytes 1806352 | tf_op jit(solution)/shard_map/psum | solution.py:21
  358.5 3.7 fusion.18
  362.7 8.8 %cholesky.59 = f32[96,96]{1,0:T(8,128)S(1)} custom-call(f32[96,96]{1,0:T(8,128)S(1)} %fusion.9), custom_call_target="Cholesky" | custom-call | tf_op jit(solution)/shard_map/jit(cholesky)/cholesky | solution.py:10
  372.2 0.7 fusion.1
  372.9 7.5 %custom-call.7 = f32[1,96,96]{1,2,0:T(8,128)S(1)} custom-call(f32[1,96,96]{2,1,0:T(8,128)S(1)} %fusion.1), custom_call_target="InvertDiagBlocksLowerTriangular" | custom-call | tf_op jit(solution)/shard_map/triangular_solve/custom-call.0 | solution.py:11
  380.8 2.0 fusion.20
  383.3 8.8 %cholesky.70 = f32[96,96]{1,0:T(8,128)S(1)} custom-call(f32[96,96]{1,0:T(8,128)S(1)} %fusion.7), custom_call_target="Cholesky" | custom-call | tf_op jit(solution)/shard_map/jit(cholesky)/cholesky | solution.py:10
  392.1 0.6 compare_reduce_fusion.1
  392.8 0.7 fusion.2
  393.4 7.4 %custom-call.8 = f32[1,96,96]{1,2,0:T(8,128)S(1)} custom-call(f32[1,96,96]{2,1,0:T(8,128)S(1)} %fusion.2), custom_call_target="InvertDiagBlocksLowerTriangular" | custom-call | tf_op jit(solution)/shard_map/triangular_solve/custom-call.0 | solution.py:11
  401.3 2.0 fusion.22
  403.7 8.8 %cholesky.81 = f32[96,96]{1,0:T(8,128)S(1)} custom-call(f32[96,96]{1,0:T(8,128)S(1)} %fusion.5), custom_call_target="Cholesky" | custom-call | tf_op jit(solution)/shard_map/jit(cholesky)/cholesky | solution.py:10
  413.2 0.7 fusion.3
  413.9 7.4 %custom-call.9 = f32[1,96,96]{1,2,0:T(8,128)S(1)} custom-call(f32[1,96,96]{2,1,0:T(8,128)S(1)} %fusion.3), custom_call_target="InvertDiagBlocksLowerTriangular" | custom-call | tf_op jit(solution)/shard_map/triangular_solve/custom-call.0 | solution.py:11
  421.2 0.7 convolution_bitcast_fusion
  421.9 0.7 copy-done.5
  422.6 9.1 %fusion.14 = f32[96,16384]{1,0:T(8,128)} fusion(f32[42,16384]{1,0:T(8,128)} %param.5, f32[672,96]{0,1:T(8,128)S(1)} %convolution_bitcast_fusion, s32[]{:T(128)S(6)} %select_n.6), kind=kOutput, calls=%fused_computation.25 | convolution fusion | flops 792723456 | bytes 9093124 | tf_op jit(solution)/shard_map/dot_general | solution.py:28
  431.8 50.0 %fusion = f32[8,16384]{1,0:T(8,128)S(1)} fusion(f32[96,16384]{1,0:T(8,128)} %fusion.14), kind=kCustom, calls=%all-reduce-scatter | all-reduce-scatter fusion | flops 2097153 | bytes 6816768
  481.8 4.4 collective-permute-start
  486.1 3.5 collective-permute-start.1
  489.7 1.9 collective-permute-start.2
  491.6 1.9 collective-permute-start.3
  494.8 53.8 %collective-permute-done.3 = f32[6,16384]{1,0:T(8,128)S(1)} collective-permute-done((f32[6,16384]{1,0:T(8,128)S(1)}, f32[6,16384]{1,0:T(8,128)S(1)}, u32[]{:S(2)}, u32[]{:S(2)}) %collective-permute-start.3) | collective-permute-done | bytes 393248
  548.6 0.8 copy-done.4
  549.6 0.8 copy-done.3
  550.4 13.8 %concatenate = f32[38,16384]{1,0:T(8,128)S(1)} concatenate(f32[6,16384]{1,0:T(8,128)} %copy-done.4, f32[8,16384]{1,0:T(8,128)} %collective-permute-done.2, f32[8,16384]{1,0:T(8,128)} %copy-done.3, f32[8,16384]{1,0:T(8,128)} %copy-done.2, f32[8,16384]{1,0:T(8,128)S(1)} %fusion), dimensions={0} | concatenate | bytes 4980736
  564.2 0.9 constant_dynamic-slice_fusion
  (35 shorter events, 5.0 us)
Async XLA Ops:
  7.2 351.4 %copy-start = (f32[672,96]{0,1:T(8,128)S(1)}, f32[672,96]{0,1:T(8,128)}, u32[]{:S(2)}) copy-start(f32[672,96]{0,1:T(8,128)} %param.6) | copy-start | bytes 774148
  7.2 351.4 %all-reduce.4.cloned.1.call-start = ((), (), s32[]{:S(2)}) async-start(), calls=%async_computation.1 | async-start | bytes 4128768 | tf_op jit(solution)/shard_map/psum | solution.py:21
  358.5 22.3 %copy-start.1 = (f32[672,672]{1,0:T(8,128)S(1)}, f32[672,672]{1,0:T(8,128)}, u32[]{:S(2)}) copy-start(f32[672,672]{1,0:T(8,128)} %all-reduce.4.cloned.1.call-done) | copy-start | bytes 5419012
  421.9 0.7 copy-start.5
  431.8 61.8 %copy-start.6 = (u32[256]{0:T(256)S(1)}, u32[256]{0:T(256)}, u32[]{:S(2)}) copy-start(u32[256]{0:T(256)} %constant.43) | copy-start | bytes 3076
  481.8 66.9 %collective-permute-start = (f32[8,16384]{1,0:T(8,128)S(1)}, f32[8,16384]{1,0:T(8,128)S(1)}, u32[]{:S(2)}, u32[]{:S(2)}) collective-permute-start(f32[8,16384]{1,0:T(8,128)S(1)} %fusion), channel_id=1, source_target_pairs={{0,16},{16,32},{32,48},{48,64},{64,80},{80,96},{96,112},{112,128},... | collective-permute-start | bytes 1572872
  486.1 62.5 %collective-permute-start.1 = (f32[8,16384]{1,0:T(8,128)S(1)}, f32[8,16384]{1,0:T(8,128)S(1)}, u32[]{:S(2)}, u32[]{:S(2)}) collective-permute-start(f32[8,16384]{1,0:T(8,128)S(1)} %fusion), channel_id=1, source_target_pairs={{0,32},{16,48},{32,64},{48,80},{64,96},{80,112},{96,128},{112,144}... | collective-permute-start | bytes 1572872
  489.7 60.8 %collective-permute-start.2 = (f32[8,16384]{1,0:T(8,128)S(1)}, f32[8,16384]{1,0:T(8,128)}, u32[]{:S(2)}, u32[]{:S(2)}) collective-permute-start(f32[8,16384]{1,0:T(8,128)S(1)} %fusion), channel_id=1, source_target_pairs={{0,48},{16,64},{32,80},{48,96},{64,112},{80,128},{96,144},{112,160... | collective-permute-start | bytes 1572872
  491.6 57.0 %collective-permute-start.3 = (f32[6,16384]{1,0:T(8,128)S(1)}, f32[6,16384]{1,0:T(8,128)S(1)}, u32[]{:S(2)}, u32[]{:S(2)}) collective-permute-start(f32[6,16384]{1,0:T(8,128)S(1)} %slice.6), channel_id=1, source_target_pairs={{0,64},{16,80},{32,96},{48,112},{64,128},{80,144},{96,160},{112,17... | collective-permute-start | bytes 1179656
  548.6 0.8 copy-start.4
  548.6 1.0 copy-start.2
  549.6 0.8 copy-start.3
Sparse Core Ops, SparseCore 0:
  99.7 258.8 all-reduce.3
where the time goes:
time: 573 us; the launch traced here: 572 us
  waiting for transfers between devices  313 us (55%)
  blocking collectives  126 us (22%)
  other arithmetic  52.6 us (9%)
  matrix products  27.5 us (5%)
  local copies, waits for them, and re-layouts  26 us (5%)
  between operations  15 us (3%)
  starting transfers between devices  11.8 us (2%)
    psum x1, waiting for transfers between devices, shards(): gram = lax.psum(partial_gram, ('fibre', 'rest'))  259 us
    all_to_all x1, blocking collectives, shards(): lax.all_to_all(slab, 'fibre', split_axis=1, concat_axis=0, tiled=True)  76.3 us
    unnamed x5, waiting for transfers between devices  53.8 us
    unnamed x1, blocking collectives  50 us
    another operation x9, other arithmetic, orthonormal(): lower = jnp.linalg.cholesky(small)  28.4 us
    another operation x6, other arithmetic, orthonormal(): lax.linalg.triangular_solve(lower, image, left_side=False, lower=True, tr...  24.2 us
    unnamed x19, local copies, waits for them, and re-layouts  21.5 us
    unnamed x4, starting transfers between devices  11.7 us
  transfers between devices with their start and end apart: 5, of which 2 were waited for; matrix products, arithmetic and copies ran while one was open for 0% of the time, Pallas kernels for 0%

commit v1 on v0

v1 whole, which is shorter than its diff:
```python
import jax
import jax.numpy as jnp
from jax import lax
from jax.experimental import pallas as pl
from jax.experimental.pallas import tpu as pltpu
from jax.sharding import PartitionSpec as P

ITERS = 3
HP = lax.Precision.HIGHEST
F32 = jnp.float32
BF16 = jnp.bfloat16
NF = 16
NR = 16
NZ = 8
ROWS = 42
I1 = 672
PAD1 = 768
RANK = 96
COLS = 16384
OWN = 1024
CHUNKS = 4
CW = OWN // CHUNKS
VMEM_LIMIT = 56 * 1024 * 1024

NT = (((1,), (1,)), ((), ()))
NN = (((1,), (0,)), ((), ()))


def split(x):
    hi = x.astype(BF16)
    lo = (x - hi.astype(F32)).astype(BF16)
    return hi, lo


def dot3(a, b, dims):
    ah, al = a
    bh, bl = b

    def d(u, v):
        return lax.dot_general(u, v, dims, preferred_element_type=F32)

    return d(ah, bh) + (d(ah, bl) + d(al, bh))


def remote(src, dst, send, recv, device):
    return pltpu.make_async_remote_copy(
        src_ref=src, dst_ref=dst, send_sem=send, recv_sem=recv,
        device_id=device, device_id_type=pl.DeviceIdType.MESH,
    )


def wrap(v, n):
    return lax.rem(v + n, n)


OFF_DIAG = [(i, j) for i in range(5) for j in range(i)]


def gram_kernel(slab, f_out, g_out, got, fc, acc, part, ra, sa, rb, own, rc, mine, full,
                s_own, s_x, r_x, s_a, r_a, s_b, r_b, s_c, r_c, s_d, r_d, s_e, r_e, s_f, r_f, s_o, s_g):
    f = lax.axis_index("fibre")
    r = lax.axis_index("rest")
    z = f // 2
    c = lax.rem(f, 2)
    other = z * 2 + (1 - c)

    barrier = pltpu.get_barrier_semaphore()
    for d in range(1, NF):
        pl.semaphore_signal(barrier, inc=1, device_id={"fibre": wrap(f + d, NF)}, device_id_type=pl.DeviceIdType.MESH)
    for d in range(1, NR):
        pl.semaphore_signal(barrier, inc=1, device_id={"rest": wrap(r + d, NR)}, device_id_type=pl.DeviceIdType.MESH)

    own_copy = pltpu.make_async_copy(slab.at[:, pl.ds(pl.multiple_of(f * OWN, OWN), OWN)], got.at[f], s_own)
    own_copy.start()
    pl.semaphore_wait(barrier, NF - 1 + NR - 1)

    def x_copy(ch, d):
        to = wrap(f + d, NF)
        return remote(
            slab.at[:, pl.ds(pl.multiple_of(to * OWN + ch * CW, CW), CW)],
            got.at[f, :, pl.ds(ch * CW, CW)],
            s_x.at[ch, d], r_x.at[ch, d], {"fibre": to},
        )

    for ch in range(CHUNKS):
        for d in range(1, NF):
            x_copy(ch, d).start()
    fc[pl.ds(I1, PAD1 - I1), :] = jnp.zeros((PAD1 - I1, OWN), F32)
    own_copy.wait()
    for ch in range(CHUNKS):
        for d in range(1, NF):
            x_copy(ch, d).wait_recv()
        cols = pl.ds(ch * CW, CW)
        for s in range(NF):
            fc[pl.ds(s * ROWS, ROWS), cols] = got[s, :, cols]
        hi, lo = split(fc[:, cols])
        for k in range(3):
            top, wide = k * 256, (k + 1) * 256
            new = dot3((hi[top:top + 256], lo[top:top + 256]), (hi[:wide], lo[:wide]), NT)
            if ch == 0:
                acc[pl.ds(top, 256), pl.ds(0, wide)] = new
            else:
                acc[pl.ds(top, 256), pl.ds(0, wide)] += new
    f_copy = pltpu.make_async_copy(fc.at[pl.ds(0, I1), :], f_out, s_o)
    f_copy.start()

    def put(b, value):
        part[b // 8, pl.ds((2 * b) % 16, 2)] = value.reshape(2, 8, 8, 128)

    def blk(i, j, rows=128):
        return acc[pl.ds(i * 128, rows), pl.ds(j * 128, 128)]

    row_id = lax.broadcasted_iota(jnp.int32, (128, 128), 0)
    col_id = lax.broadcasted_iota(jnp.int32, (128, 128), 1)
    for b, (i, j) in enumerate(OFF_DIAG):
        put(b, blk(i, j))
    second = blk(1, 1)
    put(10, jnp.where(row_id >= col_id, blk(0, 0), second))
    for k in range(2, 5):
        put(9 + k, blk(k, k))
    put(14, jnp.concatenate([blk(5, j, 32) for j in range(4)], axis=0))
    diagonal = jnp.sum(jnp.where(row_id == col_id, second, 0.0), axis=0, keepdims=True)
    put(15, jnp.concatenate(
        [blk(5, 4, 32), blk(5, 5, 32), jnp.broadcast_to(diagonal, (8, 128)), jnp.zeros((56, 128), F32)], axis=0))

    a_copy = remote(part.at[1 - c], ra, s_a, r_a, {"fibre": other})
    a_copy.start()
    a_copy.wait_recv()
    sa[...] = part[c] + ra[...]

    def b_copy(d):
        to = wrap(r + d, NR)
        return remote(sa.at[to], rb.at[d], s_b.at[d], r_b.at[d], {"rest": to})

    for d in range(1, NR):
        b_copy(d).start()
    total = sa[r]
    for d in range(1, NR):
        b_copy(d).wait_recv()
        total = total + rb[d]
    own[...] = total

    def c_copy(d):
        to = wrap(z + d, NZ)
        return remote(own.at[to], rc.at[d], s_c.at[d], r_c.at[d], {"fibre": to * 2 + c})

    for d in range(1, NZ):
        c_copy(d).start()
    tile = own[z]
    for d in range(1, NZ):
        c_copy(d).wait_recv()
        tile = tile + rc[d]
    mine[...] = tile
    full[c, r, z] = tile

    def d_copy(d):
        return remote(mine, full.at[c, r, z], s_d.at[d], r_d.at[d], {"fibre": wrap(z + d, NZ) * 2 + c})

    for d in range(1, NZ):
        d_copy(d).start()
    for d in range(1, NZ):
        d_copy(d).wait_recv()

    def e_copy(d):
        return remote(full.at[c, r], full.at[c, r], s_e.at[d], r_e.at[d], {"rest": wrap(r + d, NR)})

    def f_pass(d):
        at = wrap(r - d, NR)
        return remote(full.at[c, at], full.at[c, at], s_f.at[d], r_f.at[d], {"fibre": other})

    for d in range(1, NR):
        e_copy(d).start()
    f_pass(0).start()
    for d in range(1, NR):
        e_copy(d).wait_recv()
        f_pass(d).start()
    for d in range(NR):
        f_pass(d).wait_recv()
    g_copy = pltpu.make_async_copy(full, g_out, s_g)
    g_copy.start()

    for ch in range(CHUNKS):
        for d in range(1, NF):
            x_copy(ch, d).wait_send()
    a_copy.wait_send()
    for d in range(1, NR):
        b_copy(d).wait_send()
    for d in range(1, NZ):
        c_copy(d).wait_send()
        d_copy(d).wait_send()
    for d in range(1, NR):
        e_copy(d).wait_send()
    for d in range(NR):
        f_pass(d).wait_send()
    f_copy.wait()
    g_copy.wait()


def gram_call(slab):
    dma = pltpu.SemaphoreType.DMA
    any_spec = pl.BlockSpec(memory_space=pl.ANY)
    return pl.pallas_call(
        gram_kernel,
        out_shape=(
            jax.ShapeDtypeStruct((I1, OWN), F32),
            jax.ShapeDtypeStruct((2, NR, NZ, 8, 128), F32),
        ),
        in_specs=[any_spec],
        out_specs=(any_spec, any_spec),
        scratch_shapes=[
            pltpu.VMEM((NF, ROWS, OWN), F32),
            pltpu.VMEM((PAD1, OWN), F32),
            pltpu.VMEM((PAD1, PAD1), F32),
            pltpu.VMEM((2, NR, NZ, 8, 128), F32),
            pltpu.VMEM((NR, NZ, 8, 128), F32),
            pltpu.VMEM((NR, NZ, 8, 128), F32),
            pltpu.VMEM((NR, NZ, 8, 128), F32),
            pltpu.VMEM((NZ, 8, 128), F32),
            pltpu.VMEM((NZ, 8, 128), F32),
            pltpu.VMEM((8, 128), F32),
            pltpu.VMEM((2, NR, NZ, 8, 128), F32),
            dma,
            dma((CHUNKS, NF)), dma((CHUNKS, NF)),
            dma, dma,
            dma((NR,)), dma((NR,)),
            dma((NZ,)), dma((NZ,)),
            dma((NZ,)), dma((NZ,)),
            dma((NR,)), dma((NR,)),
            dma((NR,)), dma((NR,)),
            dma, dma,
        ],
        compiler_params=pltpu.CompilerParams(
            collective_id=0, has_side_effects=True, vmem_limit_bytes=VMEM_LIMIT),
        name="gram",
    )(slab)


def inverse_factor(small):
    tiles = [small[8 * t:8 * t + 8] for t in range(RANK // 8)]
    lane = lax.broadcasted_iota(jnp.int32, (8, 128), 1)
    sub = lax.broadcasted_iota(jnp.int32, (8, 128), 0)
    pivots = [jnp.ones((8, 128), F32) for _ in tiles]
    for j in range(RANK):
        t, i = divmod(j, 8)
        row = jnp.broadcast_to(tiles[t][i:i + 1, :], (8, 128))
        pivot = jnp.broadcast_to(row[:, j:j + 1], (8, 128))
        pivots[t] = jnp.where(sub == i, pivot, pivots[t])
        scaled = jnp.where(lane == j, 1.0, row) / pivot
        for k in range(t, len(tiles)):
            times = jnp.broadcast_to(tiles[k][:, j:j + 1], (8, 128))
            new = jnp.where(lane == j, 0.0, tiles[k]) - times * scaled
            if k == t:
                kept = jnp.where(lane == j, 1.0, tiles[k])
                new = jnp.where(sub > i, new, jnp.where(sub == i, kept, tiles[k]))
            tiles[k] = new
    tiles = [u * lax.rsqrt(p) for u, p in zip(tiles, pivots)]
    tiles = [jnp.where(lane <= sub + 8 * t, u, 0.0) for t, u in enumerate(tiles)]
    return jnp.concatenate(tiles, axis=0)


def iterate_kernel(g, start, fibres, factor, core, gh, gl, basis, fh, fl):
    row_id = lax.broadcasted_iota(jnp.int32, (128, 128), 0)
    col_id = lax.broadcasted_iota(jnp.int32, (128, 128), 1)

    def get(b):
        return g[b // 8, pl.ds((2 * b) % 16, 2)].reshape(128, 128)

    def store(i, j, value):
        hi, lo = split(value)
        at = (pl.ds(i * 128, 128), pl.ds(j * 128, 128))
        gh[at] = hi
        gl[at] = lo

    for b, (i, j) in enumerate(OFF_DIAG):
        value = get(b)
        store(i, j, value)
        store(j, i, value.T)
    for k in range(2, 5):
        store(k, k, get(9 + k))
    last = get(15)
    both = get(10)
    flip = both.T
    store(0, 0, jnp.where(row_id >= col_id, both, flip))
    diagonal = jnp.broadcast_to(last[64:65], (128, 128))
    store(1, 1, jnp.where(row_id < col_id, both, jnp.where(row_id > col_id, flip, diagonal)))
    most = get(14)
    strips = [most[32 * k:32 * k + 32] for k in range(4)] + [last[0:32], last[32:64]]
    for j, strip in enumerate(strips):
        value = jnp.concatenate([strip, jnp.zeros((96, 128), F32)], axis=0)
        store(5, j, value)
        if j < 5:
            store(j, 5, value.T)

    fh[...], fl[...] = split(fibres[...])
    basis[...] = jnp.concatenate([start[...], jnp.zeros((PAD1 - I1, RANK), F32)], axis=0).T

    def step(_, carry):
        image = dot3(split(basis[...]), (gh[...], gl[...]), NN)
        wide = jnp.concatenate([image, jnp.zeros((128 - RANK, PAD1), F32)], axis=0)
        small = lax.dot_general(image, wide, NT, precision=HP, preferred_element_type=F32)
        inverse = inverse_factor(small)[:, :RANK]
        basis[...] = lax.dot_general(inverse, image, NN, precision=HP, preferred_element_type=F32)
        return carry

    lax.fori_loop(0, ITERS, step, 0)
    last_basis = basis[...]
    factor[...] = last_basis.T[:I1]
    product = dot3(split(last_basis[:, :I1]), (fh[...], fl[...]), NN)
    for j in range(NF):
        core[j] = product[6 * j:6 * j + 6]


def iterate_call(g, start, fibres):
    vmem = pl.BlockSpec(memory_space=pltpu.VMEM)
    return pl.pallas_call(
        iterate_kernel,
        out_shape=(
            jax.ShapeDtypeStruct((I1, RANK), F32),
            jax.ShapeDtypeStruct((NF, RANK // NF, OWN), F32),
        ),
        in_specs=[vmem, vmem, vmem],
        out_specs=(vmem, vmem),
        scratch_shapes=[
            pltpu.VMEM((PAD1, PAD1), BF16),
            pltpu.VMEM((PAD1, PAD1), BF16),
            pltpu.VMEM((RANK, PAD1), F32),
            pltpu.VMEM((I1, OWN), BF16),
            pltpu.VMEM((I1, OWN), BF16),
        ],
        compiler_params=pltpu.CompilerParams(vmem_limit_bytes=VMEM_LIMIT),
        name="iterate",
    )(g, start, fibres)


def core_kernel(blocks, out, s_own, s_x, r_x):
    f = lax.axis_index("fibre")
    barrier = pltpu.get_barrier_semaphore()
    for d in range(1, NF):
        pl.semaphore_signal(barrier, inc=1, device_id={"fibre": wrap(f + d, NF)}, device_id_type=pl.DeviceIdType.MESH)
    at = pl.ds(pl.multiple_of(f * OWN, OWN), OWN)
    own_copy = pltpu.make_async_copy(blocks.at[f], out.at[:, at], s_own)
    own_copy.start()
    pl.semaphore_wait(barrier, NF - 1)

    def copy(d):
        to = wrap(f + d, NF)
        return remote(blocks.at[to], out.at[:, at], s_x.at[d], r_x.at[d], {"fibre": to})

    for d in range(1, NF):
        copy(d).start()
    own_copy.wait()
    for d in range(1, NF):
        copy(d).wait()


def core_call(blocks):
    dma = pltpu.SemaphoreType.DMA
    any_spec = pl.BlockSpec(memory_space=pl.ANY)
    return pl.pallas_call(
        core_kernel,
        out_shape=jax.ShapeDtypeStruct((RANK // NF, COLS), F32),
        in_specs=[any_spec],
        out_specs=any_spec,
        scratch_shapes=[dma, dma((NF,)), dma((NF,))],
        compiler_params=pltpu.CompilerParams(
            collective_id=1, has_side_effects=True, vmem_limit_bytes=VMEM_LIMIT),
        name="core",
    )(blocks)


def shards(slab, start_basis):
    fibres, gram = gram_call(slab)
    factor, blocks = iterate_call(gram, start_basis, fibres)
    return factor, core_call(blocks)


def solution(mesh):
    return jax.shard_map(
        shards,
        mesh=mesh,
        in_specs=(P("fibre", "rest"), P()),
        out_specs=(P(), P("fibre", "rest")),
        check_vma=False,
    )
```

time: 573 us -> 186 us (0.32)
  the two profiles are of different devices: /device:TPU:163 before, /device:TPU:1 now
where the time goes in v1:
time: 186 us
  Pallas kernels  179 us (96%)
  local copies, waits for them, and re-layouts  5.61 us (3%)
    pallas_call x1, Pallas kernels, gram_call(): pl.pallas_call(gram_kernel, out_shape=(jax.ShapeDtypeStruct((I1, OWN), F3...  114 us
    pallas_call x1, Pallas kernels, iterate_call(): pl.pallas_call(iterate_kernel, out_shape=(jax.ShapeDtypeStruct((I1, RANK)...  48.1 us
    pallas_call x1, Pallas kernels, core_call(): pl.pallas_call(core_kernel, out_shape=jax.ShapeDtypeStruct((RANK // NF, C...  17 us
    unnamed x3, local copies, waits for them, and re-layouts  5.61 us

profile of v1, /device:TPU:1, one launch (start us, length us, event | category | flops | bytes accessed | tf_op | source)
XLA Modules:
  0.0 185.6 jit_solution(10667557661602844866)
XLA Ops:
  0.6 1.9 %copy.4.start = f32[672,96]{1,0:T(8,128)} copy(f32[672,96]{0,1:T(8,128)} %param.3) | data formatting | bytes 516096 | tf_op args[1]
  2.5 114.3 %gram.1 = (f32[672,1024]{1,0:T(8,128)}, f32[2,16,8,8,128]{4,3,2,1,0:T(8,128)}) custom-call(f32[42,16384]{1,0:T(8,128)} %slab.1), custom_call_target="tpu_custom_call" | custom-call | tf_op jit(solution)/shard_map/gram/pallas_call | solution.py:202
  116.8 48.1 %iterate.1 = (f32[672,96]{1,0:T(8,128)}, f32[16,6,1024]{2,1,0:T(8,128)}) custom-call(f32[2,16,8,8,128]{4,3,2,1,0:T(8,128)} %get-tuple-element.6.g, f32[672,96]{1,0:T(8,128)} %copy.4.start, f32[672,1024]{1,0:T(8,128)} %get-tuple-element.7.fibres), custom_call_target="tpu_custom_call" | custom-call | tf_op jit(solution)/shard_map/iterate/pallas_call | solution.py:315
  164.9 1.9 copy.5
  166.8 17.0 %core.1 = f32[6,16384]{1,0:T(8,128)} custom-call(f32[16,6,1024]{2,1,0:T(8,128)} %get-tuple-element.9.blocks), custom_call_target="tpu_custom_call" | custom-call | tf_op jit(solution)/shard_map/core/pallas_call | solution.py:359
  183.7 1.9 %copy.7 = f32[6,16384]{1,0:T(8,128)} copy(f32[6,16384]{1,0:T(8,128)} %core.1) | data formatting | bytes 786432

commit v2 on v1

--- a/solution.py
+++ b/solution.py
@@ -236,26 +236,45 @@
 
 
 def inverse_factor(small):
-    tiles = [small[8 * t:8 * t + 8] for t in range(RANK // 8)]
+    count = RANK // 8
+    tiles = [small[8 * t:8 * t + 8] for t in range(count)]
     lane = lax.broadcasted_iota(jnp.int32, (8, 128), 1)
     sub = lax.broadcasted_iota(jnp.int32, (8, 128), 0)
-    pivots = [jnp.ones((8, 128), F32) for _ in tiles]
-    for j in range(RANK):
-        t, i = divmod(j, 8)
-        row = jnp.broadcast_to(tiles[t][i:i + 1, :], (8, 128))
-        pivot = jnp.broadcast_to(row[:, j:j + 1], (8, 128))
-        pivots[t] = jnp.where(sub == i, pivot, pivots[t])
-        scaled = jnp.where(lane == j, 1.0, row) / pivot
-        for k in range(t, len(tiles)):
-            times = jnp.broadcast_to(tiles[k][:, j:j + 1], (8, 128))
-            new = jnp.where(lane == j, 0.0, tiles[k]) - times * scaled
-            if k == t:
-                kept = jnp.where(lane == j, 1.0, tiles[k])
-                new = jnp.where(sub > i, new, jnp.where(sub == i, kept, tiles[k]))
-            tiles[k] = new
-    tiles = [u * lax.rsqrt(p) for u, p in zip(tiles, pivots)]
-    tiles = [jnp.where(lane <= sub + 8 * t, u, 0.0) for t, u in enumerate(tiles)]
-    return jnp.concatenate(tiles, axis=0)
+
+    def over_lanes(v, j):
+        return jnp.broadcast_to(v[:, j:j + 1], (8, 128))
+
+    def over_rows(v, k):
+        return jnp.broadcast_to(v[k:k + 1, :], (8, 128))
+
+    out = []
+    for t in range(count):
+        v = tiles[t]
+        cols = [over_lanes(v, 8 * t + k) for k in range(8)]
+        below = [[over_lanes(tiles[r], 8 * t + k) for k in range(8)] for r in range(t + 1, count)]
+        kept = jnp.zeros((8, 128), F32)
+        pivots = jnp.ones((8, 128), F32)
+        for k in range(8):
+            at = sub == k
+            here = lane == 8 * t + k
+            pivot = over_rows(cols[k], k)
+            inv = 1.0 / pivot
+            row = jnp.where(here, 1.0, over_rows(v, k))
+            kept = jnp.where(at, row, kept)
+            pivots = jnp.where(at, pivot, pivots)
+            scaled = row * inv
+            v = jnp.where(at, scaled, jnp.where(here, 0.0, v) - cols[k] * scaled)
+            for m in range(k + 1, 8):
+                entry = over_rows(cols[m], k) * inv
+                cols[m] = jnp.where(at, entry, cols[m] - cols[k] * entry)
+        rows = [over_rows(v, k) for k in range(8)]
+        block = (lane >= 8 * t) & (lane < 8 * t + 8)
+        for r in range(t + 1, count):
+            p = [below[r - t - 1][k] * rows[k] for k in range(8)]
+            total = ((p[0] + p[1]) + (p[2] + p[3])) + ((p[4] + p[5]) + (p[6] + p[7]))
+            tiles[r] = jnp.where(block, 0.0, tiles[r]) - total
+        out.append(jnp.where(lane <= sub + 8 * t, kept * lax.rsqrt(pivots), 0.0))
+    return jnp.concatenate(out, axis=0)
 
 
 def iterate_kernel(g, start, fibres, factor, core, gh, gl, basis, fh, fl):
@@ -292,7 +311,7 @@
             store(j, 5, value.T)
 
     fh[...], fl[...] = split(fibres[...])
-    basis[...] = jnp.concatenate([start[...], jnp.zeros((PAD1 - I1, RANK), F32)], axis=0).T
+    basis[...] = jnp.concatenate([start[...], jnp.zeros((RANK, PAD1 - I1), F32)], axis=1)
 
     def step(_, carry):
         image = dot3(split(basis[...]), (gh[...], gl[...]), NN)
@@ -304,7 +323,7 @@
 
     lax.fori_loop(0, ITERS, step, 0)
     last_basis = basis[...]
-    factor[...] = last_basis.T[:I1]
+    factor[...] = last_basis[:, :I1]
     product = dot3(split(last_basis[:, :I1]), (fh[...], fl[...]), NN)
     for j in range(NF):
         core[j] = product[6 * j:6 * j + 6]
@@ -315,7 +334,7 @@
     return pl.pallas_call(
         iterate_kernel,
         out_shape=(
-            jax.ShapeDtypeStruct((I1, RANK), F32),
+            jax.ShapeDtypeStruct((RANK, I1), F32),
             jax.ShapeDtypeStruct((NF, RANK // NF, OWN), F32),
         ),
         in_specs=[vmem, vmem, vmem],
@@ -370,8 +389,8 @@
 
 def shards(slab, start_basis):
     fibres, gram = gram_call(slab)
-    factor, blocks = iterate_call(gram, start_basis, fibres)
-    return factor, core_call(blocks)
+    factor, blocks = iterate_call(gram, start_basis.T, fibres)
+    return factor.T, core_call(blocks)
 
 
 def solution(mesh):

time: 186 us -> 154 us (0.83)
  Pallas kernels: 179 us -> 151 us
  local copies, waits for them, and re-layouts: 5.61 us -> 1.87 us
    pallas_call x1, Pallas kernels: 48.1 us -> 19.8 us  [iterate_call(): pl.pallas_call(iterate_kernel, out_shape=(jax.ShapeDtypeStruct((RANK, I1)...]
    unnamed x3 -> x1, local copies, waits for them, and re-layouts: 5.61 us -> 1.87 us
where the time goes in v2:
time: 154 us
  Pallas kernels  151 us (98%)
  local copies, waits for them, and re-layouts  1.87 us (1%)
    pallas_call x1, Pallas kernels, gram_call(): pl.pallas_call(gram_kernel, out_shape=(jax.ShapeDtypeStruct((I1, OWN), F3...  115 us
    pallas_call x1, Pallas kernels, iterate_call(): pl.pallas_call(iterate_kernel, out_shape=(jax.ShapeDtypeStruct((RANK, I1)...  19.8 us
    pallas_call x1, Pallas kernels, core_call(): pl.pallas_call(core_kernel, out_shape=jax.ShapeDtypeStruct((RANK // NF, C...  16.9 us

profile of v2, /device:TPU:1, one launch (start us, length us, event | category | flops | bytes accessed | tf_op | source)
XLA Modules:
  0.0 153.8 jit_solution(16613172297978162415)
XLA Ops:
  0.6 114.5 %gram.1 = (f32[672,1024]{1,0:T(8,128)}, f32[2,16,8,8,128]{4,3,2,1,0:T(8,128)}) custom-call(f32[42,16384]{1,0:T(8,128)} %slab.1), custom_call_target="tpu_custom_call" | custom-call | tf_op jit(solution)/shard_map/gram/pallas_call | solution.py:202
  115.2 19.8 %iterate.1 = (f32[96,672]{1,0:T(8,128)}, f32[16,6,1024]{2,1,0:T(8,128)}) custom-call(f32[2,16,8,8,128]{4,3,2,1,0:T(8,128)} %get-tuple-element.6.g, f32[96,672]{1,0:T(8,128)} %bitcast.2, f32[672,1024]{1,0:T(8,128)} %get-tuple-element.7.fibres), custom_call_target="tpu_custom_call" | custom-call | tf_op jit(solution)/shard_map/iterate/pallas_call | solution.py:334
  135.0 16.9 %core.1 = f32[6,16384]{1,0:T(8,128)} custom-call(f32[16,6,1024]{2,1,0:T(8,128)} %get-tuple-element.9.blocks), custom_call_target="tpu_custom_call" | custom-call | tf_op jit(solution)/shard_map/core/pallas_call | solution.py:378
  151.9 1.9 %copy.5 = f32[6,16384]{1,0:T(8,128)} copy(f32[6,16384]{1,0:T(8,128)} %core.1) | data formatting | bytes 786432

commit v3 on v2

--- a/solution.py
+++ b/solution.py
@@ -18,8 +18,6 @@
 RANK = 96
 COLS = 16384
 OWN = 1024
-CHUNKS = 4
-CW = OWN // CHUNKS
 VMEM_LIMIT = 56 * 1024 * 1024
 
 NT = (((1,), (1,)), ((), ()))
@@ -53,11 +51,20 @@
     return lax.rem(v + n, n)
 
 
-OFF_DIAG = [(i, j) for i in range(5) for j in range(i)]
-
-
-def gram_kernel(slab, f_out, g_out, got, fc, acc, part, ra, sa, rb, own, rc, mine, full,
-                s_own, s_x, r_x, s_a, r_a, s_b, r_b, s_c, r_c, s_d, r_d, s_e, r_e, s_f, r_f, s_o, s_g):
+ROW_B, ROW_C, ROW_T = 256, 512, 640
+EARLY = [(i, j) for i in range(4) for j in range(i + 1)]
+LATE = [(4, j) for j in range(5)]
+T3 = 3
+
+
+def mesh_signal(sem, device):
+    pl.semaphore_signal(sem, inc=1, device_id=device, device_id_type=pl.DeviceIdType.MESH)
+
+
+def gram_kernel(slab, f_out, g_out, g2_out, fc, fh, fl, tail, tail_out, tail_in,
+                part, ra, sa, rb, own, rc, mine, full, part2, ra2, sa2, rb2, own2, rz2, full2,
+                s_own, s_x, r_x, s_a, r_a, s_b, r_b, s_c, r_c, s_d, r_d, s_e, r_e, s_f, r_f,
+                s_a2, r_a2, s_b2, r_b2, s_c2, r_c2, s_e2, r_e2, s_f2, r_f2, s_o, s_g):
     f = lax.axis_index("fibre")
     r = lax.axis_index("rest")
     z = f // 2
@@ -66,62 +73,96 @@
 
     barrier = pltpu.get_barrier_semaphore()
     for d in range(1, NF):
-        pl.semaphore_signal(barrier, inc=1, device_id={"fibre": wrap(f + d, NF)}, device_id_type=pl.DeviceIdType.MESH)
-    for d in range(1, NR):
-        pl.semaphore_signal(barrier, inc=1, device_id={"rest": wrap(r + d, NR)}, device_id_type=pl.DeviceIdType.MESH)
-
-    own_copy = pltpu.make_async_copy(slab.at[:, pl.ds(pl.multiple_of(f * OWN, OWN), OWN)], got.at[f], s_own)
-    own_copy.start()
+        mesh_signal(barrier, {"fibre": wrap(f + d, NF)})
+    for d in range(1, NR):
+        mesh_signal(barrier, {"rest": wrap(r + d, NR)})
+
+    sets = [(0, 16, 0), (16, 16, ROW_B), (32, 8, ROW_C)]
+
+    def piece(k, to):
+        at, rows, _ = sets[k]
+        return slab.at[pl.ds(at, rows), pl.ds(pl.multiple_of(to * OWN, OWN), OWN)]
+
+    def place(k):
+        _, rows, base = sets[k]
+        return fc.at[pl.ds(pl.multiple_of(base + f * rows, rows), rows), :]
+
+    def x_copy(k, d):
+        to = wrap(f + d, NF)
+        return remote(piece(k, to), place(k), s_x.at[k, d], r_x.at[k, d], {"fibre": to})
+
+    def t_copy(d):
+        to = wrap(f + d, NF)
+        return remote(tail_out.at[to], tail_in.at[f], s_x.at[3, d], r_x.at[3, d], {"fibre": to})
+
+    tail_copy = pltpu.make_async_copy(slab.at[pl.ds(40, 2), :], tail.at[pl.ds(0, 2), :], s_own.at[3])
+    tail_copy.start()
+    own_copies = [pltpu.make_async_copy(piece(k, f), place(k), s_own.at[k]) for k in range(3)]
+    for copy in own_copies:
+        copy.start()
     pl.semaphore_wait(barrier, NF - 1 + NR - 1)
 
-    def x_copy(ch, d):
-        to = wrap(f + d, NF)
-        return remote(
-            slab.at[:, pl.ds(pl.multiple_of(to * OWN + ch * CW, CW), CW)],
-            got.at[f, :, pl.ds(ch * CW, CW)],
-            s_x.at[ch, d], r_x.at[ch, d], {"fibre": to},
-        )
-
-    for ch in range(CHUNKS):
+    for d in range(1, NF):
+        x_copy(0, d).start()
+    tail_copy.wait()
+    for to in range(NF):
+        for k in range(8):
+            both = tail[0:2, pl.ds((to * 8 + k) * 128, 128)]
+            tail_out[to, 0, k:k + 1, :] = both[0:1]
+            tail_out[to, 1, k:k + 1, :] = both[1:2]
+    tail_in[f] = tail_out[f]
+    for d in range(1, NF):
+        t_copy(d).start()
+    for k in (1, 2):
         for d in range(1, NF):
-            x_copy(ch, d).start()
-    fc[pl.ds(I1, PAD1 - I1), :] = jnp.zeros((PAD1 - I1, OWN), F32)
-    own_copy.wait()
-    for ch in range(CHUNKS):
-        for d in range(1, NF):
-            x_copy(ch, d).wait_recv()
-        cols = pl.ds(ch * CW, CW)
-        for s in range(NF):
-            fc[pl.ds(s * ROWS, ROWS), cols] = got[s, :, cols]
-        hi, lo = split(fc[:, cols])
-        for k in range(3):
-            top, wide = k * 256, (k + 1) * 256
-            new = dot3((hi[top:top + 256], lo[top:top + 256]), (hi[:wide], lo[:wide]), NT)
-            if ch == 0:
-                acc[pl.ds(top, 256), pl.ds(0, wide)] = new
-            else:
-                acc[pl.ds(top, 256), pl.ds(0, wide)] += new
-    f_copy = pltpu.make_async_copy(fc.at[pl.ds(0, I1), :], f_out, s_o)
-    f_copy.start()
+            x_copy(k, d).start()
+
+    def rounded(top, rows):
+        at = pl.ds(top, rows)
+        fh[at, :], fl[at, :] = split(fc[at, :])
+
+    def pair(top, rows):
+        return fh[pl.ds(top, rows), :], fl[pl.ds(top, rows), :]
 
     def put(b, value):
         part[b // 8, pl.ds((2 * b) % 16, 2)] = value.reshape(2, 8, 8, 128)
 
-    def blk(i, j, rows=128):
-        return acc[pl.ds(i * 128, rows), pl.ds(j * 128, 128)]
-
-    row_id = lax.broadcasted_iota(jnp.int32, (128, 128), 0)
-    col_id = lax.broadcasted_iota(jnp.int32, (128, 128), 1)
-    for b, (i, j) in enumerate(OFF_DIAG):
-        put(b, blk(i, j))
-    second = blk(1, 1)
-    put(10, jnp.where(row_id >= col_id, blk(0, 0), second))
-    for k in range(2, 5):
-        put(9 + k, blk(k, k))
-    put(14, jnp.concatenate([blk(5, j, 32) for j in range(4)], axis=0))
-    diagonal = jnp.sum(jnp.where(row_id == col_id, second, 0.0), axis=0, keepdims=True)
-    put(15, jnp.concatenate(
-        [blk(5, 4, 32), blk(5, 5, 32), jnp.broadcast_to(diagonal, (8, 128)), jnp.zeros((56, 128), F32)], axis=0))
+    def put2(tile, value):
+        for k in range(value.shape[0] // 8):
+            n = tile + k
+            part2[n // (NR * T3), (n // T3) % NR, n % T3] = value[8 * k:8 * k + 8]
+
+    fc[pl.ds(I1, PAD1 - I1), :] = jnp.zeros((PAD1 - I1, OWN), F32)
+    own_copies[0].wait()
+    for d in range(1, NF):
+        x_copy(0, d).wait_recv()
+    rounded(0, 256)
+    block = dot3(pair(0, 256), pair(0, 256), NT)
+    for b in range(3):
+        i, j = EARLY[b]
+        put(b, block[128 * i:128 * i + 128, 128 * j:128 * j + 128])
+
+    for d in range(1, NF):
+        t_copy(d).wait_recv()
+    for i in range(2):
+        for k in range(8):
+            fc[pl.ds(ROW_T + 16 * i, 16), pl.ds(128 * k, 128)] = jnp.concatenate(
+                [tail_in[s, i, k:k + 1, :] for s in range(NF)], axis=0)
+    rounded(ROW_T, PAD1 - ROW_T)
+    own_copies[1].wait()
+    for d in range(1, NF):
+        x_copy(1, d).wait_recv()
+    rounded(ROW_B, 256)
+    block = dot3(pair(ROW_B, 256), pair(0, 512), NT)
+    for b in range(3, 10):
+        i, j = EARLY[b]
+        put(b, block[128 * (i - 2):128 * (i - 2) + 128, 128 * j:128 * j + 128])
+    strip = dot3(pair(ROW_T, 32), pair(0, 512), NT)
+    put(10, jnp.concatenate([strip[:, 128 * j:128 * j + 128] for j in range(4)], axis=0))
+    corner = dot3(pair(ROW_T, 32), pair(ROW_T, 128), NT)
+    put(11, jnp.concatenate([corner, jnp.zeros((96, 128), F32)], axis=0))
+    for b in range(12, 16):
+        put(b, jnp.zeros((128, 128), F32))
 
     a_copy = remote(part.at[1 - c], ra, s_a, r_a, {"fibre": other})
     a_copy.start()
@@ -146,6 +187,21 @@
 
     for d in range(1, NZ):
         c_copy(d).start()
+
+    own_copies[2].wait()
+    for d in range(1, NF):
+        x_copy(2, d).wait_recv()
+    rounded(ROW_C, 128)
+    block = dot3(pair(ROW_C, 128), pair(0, 640), NT)
+    for j in range(5):
+        put2(16 * j, block[:, 128 * j:128 * j + 128])
+    put2(80, dot3(pair(ROW_T, 32), pair(ROW_C, 128), NT))
+    put2(84, jnp.zeros((96, 128), F32))
+    a2_copy = remote(part2.at[1 - c], ra2, s_a2, r_a2, {"fibre": other})
+    a2_copy.start()
+    f_copy = pltpu.make_async_copy(fc.at[pl.ds(0, I1), :], f_out, s_o)
+    f_copy.start()
+
     tile = own[z]
     for d in range(1, NZ):
         c_copy(d).wait_recv()
@@ -158,8 +214,16 @@
 
     for d in range(1, NZ):
         d_copy(d).start()
-    for d in range(1, NZ):
-        d_copy(d).wait_recv()
+
+    a2_copy.wait_recv()
+    sa2[...] = part2[c] + ra2[...]
+
+    def b2_copy(d):
+        to = wrap(r + d, NR)
+        return remote(sa2.at[to], rb2.at[d], s_b2.at[d], r_b2.at[d], {"rest": to})
+
+    for d in range(1, NR):
+        b2_copy(d).start()
 
     def e_copy(d):
         return remote(full.at[c, r], full.at[c, r], s_e.at[d], r_e.at[d], {"rest": wrap(r + d, NR)})
@@ -168,59 +232,105 @@
         at = wrap(r - d, NR)
         return remote(full.at[c, at], full.at[c, at], s_f.at[d], r_f.at[d], {"fibre": other})
 
+    for d in range(1, NZ):
+        d_copy(d).wait_recv()
     for d in range(1, NR):
         e_copy(d).start()
     f_pass(0).start()
+
+    total2 = sa2[r]
+    for d in range(1, NR):
+        b2_copy(d).wait_recv()
+        total2 = total2 + rb2[d]
+    own2[...] = total2
+    rz2[z] = total2
+
+    def c2_copy(d):
+        return remote(own2, rz2.at[z], s_c2.at[d], r_c2.at[d], {"fibre": wrap(z + d, NZ) * 2 + c})
+
+    for d in range(1, NZ):
+        c2_copy(d).start()
+    for d in range(1, NZ):
+        c2_copy(d).wait_recv()
+    full2[c, r] = ((rz2[0] + rz2[1]) + (rz2[2] + rz2[3])) + ((rz2[4] + rz2[5]) + (rz2[6] + rz2[7]))
+
+    def e2_copy(d):
+        return remote(full2.at[c, r], full2.at[c, r], s_e2.at[d], r_e2.at[d], {"rest": wrap(r + d, NR)})
+
+    def f2_pass(d):
+        at = wrap(r - d, NR)
+        return remote(full2.at[c, at], full2.at[c, at], s_f2.at[d], r_f2.at[d], {"fibre": other})
+
+    for d in range(1, NR):
+        e2_copy(d).start()
+    f2_pass(0).start()
+
     for d in range(1, NR):
         e_copy(d).wait_recv()
         f_pass(d).start()
+    for d in range(1, NR):
+        e2_copy(d).wait_recv()
+        f2_pass(d).start()
     for d in range(NR):
         f_pass(d).wait_recv()
-    g_copy = pltpu.make_async_copy(full, g_out, s_g)
+    g_copy = pltpu.make_async_copy(full, g_out, s_g.at[0])
     g_copy.start()
-
-    for ch in range(CHUNKS):
-        for d in range(1, NF):
-            x_copy(ch, d).wait_send()
+    for d in range(NR):
+        f2_pass(d).wait_recv()
+    g2_copy = pltpu.make_async_copy(full2, g2_out, s_g.at[1])
+    g2_copy.start()
+
+    for d in range(1, NF):
+        t_copy(d).wait_send()
+        for k in range(3):
+            x_copy(k, d).wait_send()
     a_copy.wait_send()
-    for d in range(1, NR):
-        b_copy(d).wait_send()
+    a2_copy.wait_send()
     for d in range(1, NZ):
         c_copy(d).wait_send()
         d_copy(d).wait_send()
-    for d in range(1, NR):
+        c2_copy(d).wait_send()
+    for d in range(1, NR):
+        b_copy(d).wait_send()
+        b2_copy(d).wait_send()
         e_copy(d).wait_send()
+        e2_copy(d).wait_send()
     for d in range(NR):
         f_pass(d).wait_send()
+        f2_pass(d).wait_send()
     f_copy.wait()
     g_copy.wait()
+    g2_copy.wait()
 
 
 def gram_call(slab):
     dma = pltpu.SemaphoreType.DMA
     any_spec = pl.BlockSpec(memory_space=pl.ANY)
+
+    def tiles(*shape):
+        return pltpu.VMEM((*shape, 8, 128), F32)
+
     return pl.pallas_call(
         gram_kernel,
         out_shape=(
             jax.ShapeDtypeStruct((I1, OWN), F32),
             jax.ShapeDtypeStruct((2, NR, NZ, 8, 128), F32),
+            jax.ShapeDtypeStruct((2, NR, T3, 8, 128), F32),
         ),
         in_specs=[any_spec],
-        out_specs=(any_spec, any_spec),
+        out_specs=(any_spec, any_spec, any_spec),
         scratch_shapes=[
-            pltpu.VMEM((NF, ROWS, OWN), F32),
             pltpu.VMEM((PAD1, OWN), F32),
-            pltpu.VMEM((PAD1, PAD1), F32),
-            pltpu.VMEM((2, NR, NZ, 8, 128), F32),
-            pltpu.VMEM((NR, NZ, 8, 128), F32),
-            pltpu.VMEM((NR, NZ, 8, 128), F32),
-            pltpu.VMEM((NR, NZ, 8, 128), F32),
-            pltpu.VMEM((NZ, 8, 128), F32),
-            pltpu.VMEM((NZ, 8, 128), F32),
-            pltpu.VMEM((8, 128), F32),
-            pltpu.VMEM((2, NR, NZ, 8, 128), F32),
-            dma,
-            dma((CHUNKS, NF)), dma((CHUNKS, NF)),
+            pltpu.VMEM((PAD1, OWN), BF16),
+            pltpu.VMEM((PAD1, OWN), BF16),
+            pltpu.VMEM((8, COLS), F32),
+            tiles(NF, 2), tiles(NF, 2),
+            tiles(2, NR, NZ), tiles(NR, NZ), tiles(NR, NZ), tiles(NR, NZ),
+            tiles(NZ), tiles(NZ), tiles(), tiles(2, NR, NZ),
+            tiles(2, NR, T3), tiles(NR, T3), tiles(NR, T3), tiles(NR, T3),
+            tiles(T3), tiles(NZ, T3), tiles(2, NR, T3),
+            dma((4,)),
+            dma((4, NF)), dma((4, NF)),
             dma, dma,
             dma((NR,)), dma((NR,)),
             dma((NZ,)), dma((NZ,)),
@@ -228,6 +338,11 @@
             dma((NR,)), dma((NR,)),
             dma((NR,)), dma((NR,)),
             dma, dma,
+            dma((NR,)), dma((NR,)),
+            dma((NZ,)), dma((NZ,)),
+            dma((NR,)), dma((NR,)),
+            dma((NR,)), dma((NR,)),
+            dma, dma((2,)),
         ],
         compiler_params=pltpu.CompilerParams(
             collective_id=0, has_side_effects=True, vmem_limit_bytes=VMEM_LIMIT),
@@ -277,12 +392,36 @@
     return jnp.concatenate(out, axis=0)
 
 
-def iterate_kernel(g, start, fibres, factor, core, gh, gl, basis, fh, fl):
-    row_id = lax.broadcasted_iota(jnp.int32, (128, 128), 0)
-    col_id = lax.broadcasted_iota(jnp.int32, (128, 128), 1)
-
+def permutation(transposed):
+    p = lax.broadcasted_iota(jnp.int32, (PAD1, PAD1), 0 if transposed else 1)
+    i = lax.broadcasted_iota(jnp.int32, (PAD1, PAD1), 1 if transposed else 0)
+    q = p - ROW_T
+    wide = ROWS * ((p & 255) >> 4) + (p & 15) + jnp.where(p >= ROW_B, 16, 0)
+    narrow = ROWS * ((p - ROW_C) >> 3) + 32 + (p & 7)
+    rest = ROWS * (q & 15) + 40 + (q >> 4)
+    row = jnp.where(p < ROW_C, wide, jnp.where(p < ROW_T, narrow, jnp.where(p < I1, rest, p)))
+    return jnp.where(row == i, 1.0, 0.0).astype(BF16)
+
+
+def permuted(x, ones):
+    hi = x.astype(BF16)
+    left = x - hi.astype(F32)
+    mid = left.astype(BF16)
+    low = (left - mid.astype(F32)).astype(BF16)
+
+    def d(u):
+        return lax.dot_general(u, ones, NN, preferred_element_type=F32)
+
+    return d(hi) + (d(mid) + d(low))
+
+
+def iterate_kernel(g, g2, start, fibres, factor, core, gh, gl, basis, fh, fl):
     def get(b):
         return g[b // 8, pl.ds((2 * b) % 16, 2)].reshape(128, 128)
+
+    def get2(tile, count):
+        at = range(tile, tile + count)
+        return jnp.concatenate([g2[n // (NR * T3), (n // T3) % NR, n % T3] for n in at], axis=0)
 
     def store(i, j, value):
         hi, lo = split(value)
@@ -290,28 +429,27 @@
         gh[at] = hi
         gl[at] = lo
 
-    for b, (i, j) in enumerate(OFF_DIAG):
-        value = get(b)
+    def store_both(i, j, value):
         store(i, j, value)
-        store(j, i, value.T)
-    for k in range(2, 5):
-        store(k, k, get(9 + k))
-    last = get(15)
-    both = get(10)
-    flip = both.T
-    store(0, 0, jnp.where(row_id >= col_id, both, flip))
-    diagonal = jnp.broadcast_to(last[64:65], (128, 128))
-    store(1, 1, jnp.where(row_id < col_id, both, jnp.where(row_id > col_id, flip, diagonal)))
-    most = get(14)
-    strips = [most[32 * k:32 * k + 32] for k in range(4)] + [last[0:32], last[32:64]]
-    for j, strip in enumerate(strips):
-        value = jnp.concatenate([strip, jnp.zeros((96, 128), F32)], axis=0)
-        store(5, j, value)
-        if j < 5:
-            store(j, 5, value.T)
+        if i != j:
+            store(j, i, value.T)
+
+    def deep(strip):
+        return jnp.concatenate([strip, jnp.zeros((96, 128), F32)], axis=0)
+
+    for b, (i, j) in enumerate(EARLY):
+        store_both(i, j, get(b))
+    strips = get(10)
+    for j in range(4):
+        store_both(5, j, deep(strips[32 * j:32 * j + 32]))
+    store(5, 5, get(11))
+    for j in range(5):
+        store_both(4, j, get2(16 * j, 16))
+    store_both(5, 4, deep(get2(80, 4)))
 
     fh[...], fl[...] = split(fibres[...])
-    basis[...] = jnp.concatenate([start[...], jnp.zeros((RANK, PAD1 - I1), F32)], axis=1)
+    wide_start = jnp.concatenate([start[...], jnp.zeros((RANK, PAD1 - I1), F32)], axis=1)
+    basis[...] = permuted(wide_start, permutation(False))
 
     def step(_, carry):
         image = dot3(split(basis[...]), (gh[...], gl[...]), NN)
@@ -323,13 +461,13 @@
 
     lax.fori_loop(0, ITERS, step, 0)
     last_basis = basis[...]
-    factor[...] = last_basis[:, :I1]
+    factor[...] = permuted(last_basis, permutation(True))[:, :I1]
     product = dot3(split(last_basis[:, :I1]), (fh[...], fl[...]), NN)
     for j in range(NF):
         core[j] = product[6 * j:6 * j + 6]
 
 
-def iterate_call(g, start, fibres):
+def iterate_call(g, g2, start, fibres):
     vmem = pl.BlockSpec(memory_space=pltpu.VMEM)
     return pl.pallas_call(
         iterate_kernel,
@@ -337,7 +475,7 @@
             jax.ShapeDtypeStruct((RANK, I1), F32),
             jax.ShapeDtypeStruct((NF, RANK // NF, OWN), F32),
         ),
-        in_specs=[vmem, vmem, vmem],
+        in_specs=[vmem, vmem, vmem, vmem],
         out_specs=(vmem, vmem),
         scratch_shapes=[
             pltpu.VMEM((PAD1, PAD1), BF16),
@@ -348,7 +486,7 @@
         ],
         compiler_params=pltpu.CompilerParams(vmem_limit_bytes=VMEM_LIMIT),
         name="iterate",
-    )(g, start, fibres)
+    )(g, g2, start, fibres)
 
 
 def core_kernel(blocks, out, s_own, s_x, r_x):
@@ -388,8 +526,8 @@
 
 
 def shards(slab, start_basis):
-    fibres, gram = gram_call(slab)
-    factor, blocks = iterate_call(gram, start_basis.T, fibres)
+    fibres, gram, gram2 = gram_call(slab)
+    factor, blocks = iterate_call(gram, gram2, start_basis.T, fibres)
     return factor.T, core_call(blocks)
 
 

time: 154 us -> 144 us (0.935)
  Pallas kernels: 151 us -> 141 us
    pallas_call x1, Pallas kernels: 115 us -> 103 us  [gram_call(): pl.pallas_call(gram_kernel, out_shape=(jax.ShapeDtypeStruct((I1, OWN), F3...]
where the time goes in v3:
time: 144 us
  Pallas kernels  141 us (98%)
  local copies, waits for them, and re-layouts  1.87 us (1%)
    pallas_call x1, Pallas kernels, gram_call(): pl.pallas_call(gram_kernel, out_shape=(jax.ShapeDtypeStruct((I1, OWN), F3...  103 us
    pallas_call x1, Pallas kernels, iterate_call(): pl.pallas_call(iterate_kernel, out_shape=(jax.ShapeDtypeStruct((RANK, I1)...  21.1 us
    pallas_call x1, Pallas kernels, core_call(): pl.pallas_call(core_kernel, out_shape=jax.ShapeDtypeStruct((RANK // NF, C...  17.5 us

profile of v3, /device:TPU:1, one launch (start us, length us, event | category | flops | bytes accessed | tf_op | source)
XLA Modules:
  0.0 143.9 jit_solution(814460263880140868)
XLA Ops:
  0.6 102.8 %gram.1 = (f32[672,1024]{1,0:T(8,128)}, f32[2,16,8,8,128]{4,3,2,1,0:T(8,128)}, f32[2,16,3,8,128]{4,3,2,1,0:T(8,128)}) custom-call(f32[42,16384]{1,0:T(8,128)} %slab.1), custom_call_target="tpu_custom_call" | custom-call | tf_op jit(solution)/shard_map/gram/pallas_call | solution.py:313
  103.5 21.1 %iterate.1 = (f32[96,672]{1,0:T(8,128)}, f32[16,6,1024]{2,1,0:T(8,128)}) custom-call(f32[2,16,8,8,128]{4,3,2,1,0:T(8,128)} %get-tuple-element.7.g, f32[2,16,3,8,128]{4,3,2,1,0:T(8,128)} %get-tuple-element.8.g2, f32[96,672]{1,0:T(8,128)} %bitcast.2, f32[672,1024]{1,0:T(8,128)} %get-tuple-element.9.fibres), custom_call_target="tpu_custom_call" | custom-call | tf_op jit(solution)/shard_map/iterate/pallas_call | solution.py:472
  124.6 17.5 %core.1 = f32[6,16384]{1,0:T(8,128)} custom-call(f32[16,6,1024]{2,1,0:T(8,128)} %get-tuple-element.11.blocks), custom_call_target="tpu_custom_call" | custom-call | tf_op jit(solution)/shard_map/core/pallas_call | solution.py:516
  142.1 1.9 %copy.5 = f32[6,16384]{1,0:T(8,128)} copy(f32[6,16384]{1,0:T(8,128)} %core.1) | data formatting | bytes 786432

commit v4 on v3

v4 whole, which is shorter than its diff:
```python
import jax
import jax.numpy as jnp
from jax import lax
from jax.experimental import pallas as pl
from jax.experimental.pallas import tpu as pltpu
from jax.sharding import PartitionSpec as P

ITERS = 3
HP = lax.Precision.HIGHEST
F32 = jnp.float32
BF16 = jnp.bfloat16
NF = 16
NR = 16
NZ = 8
ROWS = 42
I1 = 672
PAD1 = 768
RANK = 96
COLS = 16384
OWN = 1024
VMEM_LIMIT = 56 * 1024 * 1024

NT = (((1,), (1,)), ((), ()))
NN = (((1,), (0,)), ((), ()))


def split(x):
    hi = x.astype(BF16)
    lo = (x - hi.astype(F32)).astype(BF16)
    return hi, lo


def dot3(a, b, dims):
    ah, al = a
    bh, bl = b

    def d(u, v):
        return lax.dot_general(u, v, dims, preferred_element_type=F32)

    return d(ah, bh) + (d(ah, bl) + d(al, bh))


def remote(src, dst, send, recv, device):
    return pltpu.make_async_remote_copy(
        src_ref=src, dst_ref=dst, send_sem=send, recv_sem=recv,
        device_id=device, device_id_type=pl.DeviceIdType.MESH,
    )


def wrap(v, n):
    return lax.rem(v + n, n)


def inverse_factor(small):
    count = RANK // 8
    tiles = [small[8 * t:8 * t + 8] for t in range(count)]
    lane = lax.broadcasted_iota(jnp.int32, (8, 128), 1)
    sub = lax.broadcasted_iota(jnp.int32, (8, 128), 0)

    def over_lanes(v, j):
        return jnp.broadcast_to(v[:, j:j + 1], (8, 128))

    def over_rows(v, k):
        return jnp.broadcast_to(v[k:k + 1, :], (8, 128))

    out = []
    for t in range(count):
        v = tiles[t]
        cols = [over_lanes(v, 8 * t + k) for k in range(8)]
        below = [[over_lanes(tiles[r], 8 * t + k) for k in range(8)] for r in range(t + 1, count)]
        kept = jnp.zeros((8, 128), F32)
        pivots = jnp.ones((8, 128), F32)
        for k in range(8):
            at = sub == k
            here = lane == 8 * t + k
            pivot = over_rows(cols[k], k)
            inv = 1.0 / pivot
            row = jnp.where(here, 1.0, over_rows(v, k))
            kept = jnp.where(at, row, kept)
            pivots = jnp.where(at, pivot, pivots)
            scaled = row * inv
            v = jnp.where(at, scaled, jnp.where(here, 0.0, v) - cols[k] * scaled)
            for m in range(k + 1, 8):
                entry = over_rows(cols[m], k) * inv
                cols[m] = jnp.where(at, entry, cols[m] - cols[k] * entry)
        rows = [over_rows(v, k) for k in range(8)]
        block = (lane >= 8 * t) & (lane < 8 * t + 8)
        for r in range(t + 1, count):
            p = [below[r - t - 1][k] * rows[k] for k in range(8)]
            total = ((p[0] + p[1]) + (p[2] + p[3])) + ((p[4] + p[5]) + (p[6] + p[7]))
            tiles[r] = jnp.where(block, 0.0, tiles[r]) - total
        out.append(jnp.where(lane <= sub + 8 * t, kept * lax.rsqrt(pivots), 0.0))
    return jnp.concatenate(out, axis=0)


def permutation(transposed):
    p = lax.broadcasted_iota(jnp.int32, (PAD1, PAD1), 0 if transposed else 1)
    i = lax.broadcasted_iota(jnp.int32, (PAD1, PAD1), 1 if transposed else 0)
    q = p - ROW_T
    wide = ROWS * ((p & 255) >> 4) + (p & 15) + jnp.where(p >= ROW_B, 16, 0)
    narrow = ROWS * ((p - ROW_C) >> 3) + 32 + (p & 7)
    rest = ROWS * (q & 15) + 40 + (q >> 4)
    row = jnp.where(p < ROW_C, wide, jnp.where(p < ROW_T, narrow, jnp.where(p < I1, rest, p)))
    return jnp.where(row == i, 1.0, 0.0).astype(BF16)


def permuted(x, ones):
    hi = x.astype(BF16)
    left = x - hi.astype(F32)
    mid = left.astype(BF16)
    low = (left - mid.astype(F32)).astype(BF16)

    def d(u):
        return lax.dot_general(u, ones, NN, preferred_element_type=F32)

    return d(hi) + (d(mid) + d(low))


ROW_B, ROW_C, ROW_T = 256, 512, 640
EARLY = [(i, j) for i in range(4) for j in range(i + 1)]
LATE = [(4, j) for j in range(5)]
T3 = 3


def mesh_signal(sem, device):
    pl.semaphore_signal(sem, inc=1, device_id=device, device_id_type=pl.DeviceIdType.MESH)


def main_kernel(slab, start, factor, core, fc, fh, fl, tail, tail_out, tail_in, gh, gl, basis, turned, core_tiles,
                part, ra, sa, rb, own, rc, mine, full, part2, ra2, sa2, rb2, own2, rz2, full2,
                s_own, s_x, r_x, s_a, r_a, s_b, r_b, s_c, r_c, s_d, r_d, s_e, r_e, s_f, r_f,
                s_a2, r_a2, s_b2, r_b2, s_c2, r_c2, s_e2, r_e2, s_f2, r_f2, s_z, r_z, s_o):
    f = lax.axis_index("fibre")
    r = lax.axis_index("rest")
    z = f // 2
    c = lax.rem(f, 2)
    other = z * 2 + (1 - c)

    barrier = pltpu.get_barrier_semaphore()
    for d in range(1, NF):
        mesh_signal(barrier, {"fibre": wrap(f + d, NF)})
    for d in range(1, NR):
        mesh_signal(barrier, {"rest": wrap(r + d, NR)})

    sets = [(0, 16, 0), (16, 16, ROW_B), (32, 8, ROW_C)]

    def piece(k, to):
        at, rows, _ = sets[k]
        return slab.at[pl.ds(at, rows), pl.ds(pl.multiple_of(to * OWN, OWN), OWN)]

    def place(k):
        _, rows, base = sets[k]
        return fc.at[pl.ds(pl.multiple_of(base + f * rows, rows), rows), :]

    def x_copy(k, d):
        to = wrap(f + d, NF)
        return remote(piece(k, to), place(k), s_x.at[k, d], r_x.at[k, d], {"fibre": to})

    def t_copy(d):
        to = wrap(f + d, NF)
        return remote(tail_out.at[to], tail_in.at[f], s_x.at[3, d], r_x.at[3, d], {"fibre": to})

    tail_copy = pltpu.make_async_copy(slab.at[pl.ds(40, 2), :], tail.at[pl.ds(0, 2), :], s_own.at[3])
    tail_copy.start()
    own_copies = [pltpu.make_async_copy(piece(k, f), place(k), s_own.at[k]) for k in range(3)]
    for copy in own_copies:
        copy.start()
    pl.semaphore_wait(barrier, NF - 1 + NR - 1)

    for d in range(1, NF):
        x_copy(0, d).start()
    tail_copy.wait()
    for to in range(NF):
        for k in range(8):
            both = tail[0:2, pl.ds((to * 8 + k) * 128, 128)]
            tail_out[to, 0, k:k + 1, :] = both[0:1]
            tail_out[to, 1, k:k + 1, :] = both[1:2]
    tail_in[f] = tail_out[f]
    for d in range(1, NF):
        t_copy(d).start()
    for k in (1, 2):
        for d in range(1, NF):
            x_copy(k, d).start()

    def rounded(top, rows):
        at = pl.ds(top, rows)
        fh[at, :], fl[at, :] = split(fc[at, :])

    def pair(top, rows):
        return fh[pl.ds(top, rows), :], fl[pl.ds(top, rows), :]

    def put(b, value):
        part[b // 8, pl.ds((2 * b) % 16, 2)] = value.reshape(2, 8, 8, 128)

    def put2(tile, value):
        for k in range(value.shape[0] // 8):
            n = tile + k
            part2[n // (NR * T3), (n // T3) % NR, n % T3] = value[8 * k:8 * k + 8]

    fc[pl.ds(I1, PAD1 - I1), :] = jnp.zeros((PAD1 - I1, OWN), F32)
    wide_start = jnp.concatenate([start[...], jnp.zeros((RANK, PAD1 - I1), F32)], axis=1)
    basis[...] = permuted(wide_start, permutation(False))
    own_copies[0].wait()
    for d in range(1, NF):
        x_copy(0, d).wait_recv()
    rounded(0, 256)
    block = dot3(pair(0, 256), pair(0, 256), NT)
    for b in range(3):
        i, j = EARLY[b]
        put(b, block[128 * i:128 * i + 128, 128 * j:128 * j + 128])

    for d in range(1, NF):
        t_copy(d).wait_recv()
    for i in range(2):
        for k in range(8):
            fc[pl.ds(ROW_T + 16 * i, 16), pl.ds(128 * k, 128)] = jnp.concatenate(
                [tail_in[s, i, k:k + 1, :] for s in range(NF)], axis=0)
    rounded(ROW_T, PAD1 - ROW_T)
    own_copies[1].wait()
    for d in range(1, NF):
        x_copy(1, d).wait_recv()
    rounded(ROW_B, 256)
    block = dot3(pair(ROW_B, 256), pair(0, 512), NT)
    for b in range(3, 10):
        i, j = EARLY[b]
        put(b, block[128 * (i - 2):128 * (i - 2) + 128, 128 * j:128 * j + 128])
    strip = dot3(pair(ROW_T, 32), pair(0, 512), NT)
    put(10, jnp.concatenate([strip[:, 128 * j:128 * j + 128] for j in range(4)], axis=0))
    corner = dot3(pair(ROW_T, 32), pair(ROW_T, 128), NT)
    put(11, jnp.concatenate([corner, jnp.zeros((96, 128), F32)], axis=0))
    for b in range(12, 16):
        put(b, jnp.zeros((128, 128), F32))

    a_copy = remote(part.at[1 - c], ra, s_a, r_a, {"fibre": other})
    a_copy.start()
    a_copy.wait_recv()
    sa[...] = part[c] + ra[...]

    def b_copy(d):
        to = wrap(r + d, NR)
        return remote(sa.at[to], rb.at[d], s_b.at[d], r_b.at[d], {"rest": to})

    for d in range(1, NR):
        b_copy(d).start()
    total = sa[r]
    for d in range(1, NR):
        b_copy(d).wait_recv()
        total = total + rb[d]
    own[...] = total

    def c_copy(d):
        to = wrap(z + d, NZ)
        return remote(own.at[to], rc.at[d], s_c.at[d], r_c.at[d], {"fibre": to * 2 + c})

    for d in range(1, NZ):
        c_copy(d).start()

    own_copies[2].wait()
    for d in range(1, NF):
        x_copy(2, d).wait_recv()
    rounded(ROW_C, 128)
    block = dot3(pair(ROW_C, 128), pair(0, 640), NT)
    for j in range(5):
        put2(16 * j, block[:, 128 * j:128 * j + 128])
    put2(80, dot3(pair(ROW_T, 32), pair(ROW_C, 128), NT))
    put2(84, jnp.zeros((96, 128), F32))
    a2_copy = remote(part2.at[1 - c], ra2, s_a2, r_a2, {"fibre": other})
    a2_copy.start()

    tile = own[z]
    for d in range(1, NZ):
        c_copy(d).wait_recv()
        tile = tile + rc[d]
    mine[...] = tile
    full[c, r, z] = tile

    def d_copy(d):
        return remote(mine, full.at[c, r, z], s_d.at[d], r_d.at[d], {"fibre": wrap(z + d, NZ) * 2 + c})

    for d in range(1, NZ):
        d_copy(d).start()

    a2_copy.wait_recv()
    sa2[...] = part2[c] + ra2[...]

    def b2_copy(d):
        to = wrap(r + d, NR)
        return remote(sa2.at[to], rb2.at[d], s_b2.at[d], r_b2.at[d], {"rest": to})

    for d in range(1, NR):
        b2_copy(d).start()

    def e_copy(d):
        return remote(full.at[c, r], full.at[c, r], s_e.at[d], r_e.at[d], {"rest": wrap(r + d, NR)})

    def f_pass(d):
        at = wrap(r - d, NR)
        return remote(full.at[c, at], full.at[c, at], s_f.at[d], r_f.at[d], {"fibre": other})

    for d in range(1, NZ):
        d_copy(d).wait_recv()
    for d in range(1, NR):
        e_copy(d).start()
    f_pass(0).start()

    total2 = sa2[r]
    for d in range(1, NR):
        b2_copy(d).wait_recv()
        total2 = total2 + rb2[d]
    own2[...] = total2
    rz2[z] = total2

    def c2_copy(d):
        return remote(own2, rz2.at[z], s_c2.at[d], r_c2.at[d], {"fibre": wrap(z + d, NZ) * 2 + c})

    for d in range(1, NZ):
        c2_copy(d).start()
    for d in range(1, NZ):
        c2_copy(d).wait_recv()
    full2[c, r] = ((rz2[0] + rz2[1]) + (rz2[2] + rz2[3])) + ((rz2[4] + rz2[5]) + (rz2[6] + rz2[7]))

    def e2_copy(d):
        return remote(full2.at[c, r], full2.at[c, r], s_e2.at[d], r_e2.at[d], {"rest": wrap(r + d, NR)})

    def f2_pass(d):
        at = wrap(r - d, NR)
        return remote(full2.at[c, at], full2.at[c, at], s_f2.at[d], r_f2.at[d], {"fibre": other})

    for d in range(1, NR):
        e2_copy(d).start()
    f2_pass(0).start()

    for d in range(1, NR):
        e_copy(d).wait_recv()
        f_pass(d).start()
    for d in range(NR):
        f_pass(d).wait_recv()

    def store(i, j, value):
        hi, lo = split(value)
        at = (pl.ds(i * 128, 128), pl.ds(j * 128, 128))
        gh[at] = hi
        gl[at] = lo

    def store_both(i, j, value):
        store(i, j, value)
        if i != j:
            store(j, i, value.T)

    def get(b):
        return full[b // 8, pl.ds((2 * b) % 16, 2)].reshape(128, 128)

    def get2(tile, count):
        at = range(tile, tile + count)
        return jnp.concatenate([full2[n // (NR * T3), (n // T3) % NR, n % T3] for n in at], axis=0)

    def deep(value):
        return jnp.concatenate([value, jnp.zeros((96, 128), F32)], axis=0)

    for b, (i, j) in enumerate(EARLY):
        store_both(i, j, get(b))
    strips = get(10)
    for j in range(4):
        store_both(5, j, deep(strips[32 * j:32 * j + 32]))
    store(5, 5, get(11))

    for d in range(1, NR):
        e2_copy(d).wait_recv()
        f2_pass(d).start()
    for d in range(NR):
        f2_pass(d).wait_recv()
    for j in range(5):
        store_both(4, j, get2(16 * j, 16))
    store_both(5, 4, deep(get2(80, 4)))

    def step(_, carry):
        image = dot3(split(basis[...]), (gh[...], gl[...]), NN)
        wide = jnp.concatenate([image, jnp.zeros((128 - RANK, PAD1), F32)], axis=0)
        small = lax.dot_general(image, wide, NT, precision=HP, preferred_element_type=F32)
        inverse = inverse_factor(small)[:, :RANK]
        basis[...] = lax.dot_general(inverse, image, NN, precision=HP, preferred_element_type=F32)
        return carry

    lax.fori_loop(0, ITERS, step, 0)

    product = dot3(split(basis[...]), (fh[...], fl[...]), NN)
    for k in range(8):
        core_tiles[pl.ds(k, RANK, stride=8), :] = product[:, 128 * k:128 * k + 128]

    def z_copy(d):
        to = wrap(f + d, NF)
        return remote(core_tiles.at[pl.ds(pl.multiple_of(to * 48, 8), 48), :],
                      core.at[pl.ds(pl.multiple_of(f * 48, 8), 48), :],
                      s_z.at[d], r_z.at[d], {"fibre": to})

    for d in range(1, NF):
        z_copy(d).start()
    own_at = pl.ds(pl.multiple_of(f * 48, 8), 48)
    core_copy = pltpu.make_async_copy(core_tiles.at[own_at, :], core.at[own_at, :], s_o.at[0])
    core_copy.start()
    turned[...] = permuted(basis[...], permutation(True))[:, :I1]
    factor_copy = pltpu.make_async_copy(turned, factor, s_o.at[1])
    factor_copy.start()

    for d in range(1, NF):
        t_copy(d).wait_send()
        for k in range(3):
            x_copy(k, d).wait_send()
    a_copy.wait_send()
    a2_copy.wait_send()
    for d in range(1, NZ):
        c_copy(d).wait_send()
        d_copy(d).wait_send()
        c2_copy(d).wait_send()
    for d in range(1, NR):
        b_copy(d).wait_send()
        b2_copy(d).wait_send()
        e_copy(d).wait_send()
        e2_copy(d).wait_send()
    for d in range(NR):
        f_pass(d).wait_send()
        f2_pass(d).wait_send()
    for d in range(1, NF):
        z_copy(d).wait()
    core_copy.wait()
    factor_copy.wait()


def main_call(slab, start):
    dma = pltpu.SemaphoreType.DMA
    any_spec = pl.BlockSpec(memory_space=pl.ANY)

    def tiles(*shape):
        return pltpu.VMEM((*shape, 8, 128), F32)

    return pl.pallas_call(
        main_kernel,
        out_shape=(
            jax.ShapeDtypeStruct((RANK, I1), F32),
            jax.ShapeDtypeStruct((RANK * 8, 128), F32),
        ),
        in_specs=[any_spec, pl.BlockSpec(memory_space=pltpu.VMEM)],
        out_specs=(any_spec, any_spec),
        scratch_shapes=[
            pltpu.VMEM((PAD1, OWN), F32),
            pltpu.VMEM((PAD1, OWN), BF16),
            pltpu.VMEM((PAD1, OWN), BF16),
            pltpu.VMEM((8, COLS), F32),
            tiles(NF, 2), tiles(NF, 2),
            pltpu.VMEM((PAD1, PAD1), BF16),
            pltpu.VMEM((PAD1, PAD1), BF16),
            pltpu.VMEM((RANK, PAD1), F32),
            pltpu.VMEM((RANK, I1), F32),
            pltpu.VMEM((RANK * 8, 128), F32),
            tiles(2, NR, NZ), tiles(NR, NZ), tiles(NR, NZ), tiles(NR, NZ),
            tiles(NZ), tiles(NZ), tiles(), tiles(2, NR, NZ),
            tiles(2, NR, T3), tiles(NR, T3), tiles(NR, T3), tiles(NR, T3),
            tiles(T3), tiles(NZ, T3), tiles(2, NR, T3),
            dma((4,)),
            dma((4, NF)), dma((4, NF)),
            dma, dma,
            dma((NR,)), dma((NR,)),
            dma((NZ,)), dma((NZ,)),
            dma((NZ,)), dma((NZ,)),
            dma((NR,)), dma((NR,)),
            dma((NR,)), dma((NR,)),
            dma, dma,
            dma((NR,)), dma((NR,)),
            dma((NZ,)), dma((NZ,)),
            dma((NR,)), dma((NR,)),
            dma((NR,)), dma((NR,)),
            dma((NF,)), dma((NF,)),
            dma((2,)),
        ],
        compiler_params=pltpu.CompilerParams(
            collective_id=0, has_side_effects=True, vmem_limit_bytes=VMEM_LIMIT),
        name="main",
    )(slab, start)


def layout_kernel(turned, tiles, factor, core):
    factor[...] = turned[...]
    for s in range(NF):
        for k in range(8):
            core[:, pl.ds((8 * s + k) * 128, 128)] = tiles[pl.ds(48 * s + k, RANK // NF, stride=8), :]


def layout_call(turned, tiles):
    vmem = pl.BlockSpec(memory_space=pltpu.VMEM)
    return pl.pallas_call(
        layout_kernel,
        out_shape=(
            jax.ShapeDtypeStruct((RANK, I1), F32),
            jax.ShapeDtypeStruct((RANK // NF, COLS), F32),
        ),
        in_specs=[vmem, vmem],
        out_specs=(vmem, vmem),
        compiler_params=pltpu.CompilerParams(vmem_limit_bytes=VMEM_LIMIT),
        name="layout",
    )(turned, tiles)


def shards(slab, start_basis):
    factor, core = layout_call(*main_call(slab, start_basis.T))
    return factor.T, core


def solution(mesh):
    return jax.shard_map(
        shards,
        mesh=mesh,
        in_specs=(P("fibre", "rest"), P()),
        out_specs=(P(), P("fibre", "rest")),
        check_vma=False,
    )
```

time: 144 us -> 133 us (0.924)
  Pallas kernels: 141 us -> 132 us
  local copies, waits for them, and re-layouts: 1.87 us -> 0 us
    pallas_call x3 -> x2, Pallas kernels: 141 us -> 132 us  [the longest x1 130 us: main_call(): pl.pallas_call(main_kernel, out_shape=(jax.ShapeDtypeStruct((RANK, I1), F...]
    unnamed x1 -> x0, local copies, waits for them, and re-layouts: 1.87 us -> none
where the time goes in v4:
time: 133 us
  Pallas kernels  132 us (99%)
    pallas_call x1, Pallas kernels, main_call(): pl.pallas_call(main_kernel, out_shape=(jax.ShapeDtypeStruct((RANK, I1), F...  130 us

profile of v4, /device:TPU:1, one launch (start us, length us, event | category | flops | bytes accessed | tf_op | source)
XLA Modules:
  0.0 132.8 jit_solution(5523167721959231186)
XLA Ops:
  0.6 130.1 %main.1 = (f32[96,672]{1,0:T(8,128)}, f32[768,128]{1,0:T(8,128)}) custom-call(f32[42,16384]{1,0:T(8,128)} %slab.1, f32[96,672]{1,0:T(8,128)} %bitcast.2), custom_call_target="tpu_custom_call" | custom-call | tf_op jit(solution)/shard_map/main/pallas_call | solution.py:436
  130.7 2.1 %layout.1 = (f32[96,672]{1,0:T(8,128)}, f32[6,16384]{1,0:T(8,128)}) custom-call(f32[96,672]{1,0:T(8,128)} %get-tuple-element.6.turned, f32[768,128]{1,0:T(8,128)} %get-tuple-element.7.tiles), custom_call_target="tpu_custom_call" | custom-call | tf_op jit(solution)/shard_map/layout/pallas_call | solution.py:490

commit v5 on v4

v5 whole, which is shorter than its diff:
```python
import jax
import jax.numpy as jnp
from jax import lax
from jax.experimental import pallas as pl
from jax.experimental.pallas import tpu as pltpu
from jax.sharding import PartitionSpec as P

ITERS = 3
HP = lax.Precision.HIGHEST
F32 = jnp.float32
BF16 = jnp.bfloat16
NF = 16
NR = 16
NZ = 8
ROWS = 42
I1 = 672
PAD1 = 768
RANK = 96
COLS = 16384
OWN = 1024
VMEM_LIMIT = 56 * 1024 * 1024

NT = (((1,), (1,)), ((), ()))
NN = (((1,), (0,)), ((), ()))


def split(x):
    hi = x.astype(BF16)
    lo = (x - hi.astype(F32)).astype(BF16)
    return hi, lo


def dot3(a, b, dims):
    ah, al = a
    bh, bl = b

    def d(u, v):
        return lax.dot_general(u, v, dims, preferred_element_type=F32)

    return d(ah, bh) + (d(ah, bl) + d(al, bh))


def remote(src, dst, send, recv, device):
    return pltpu.make_async_remote_copy(
        src_ref=src, dst_ref=dst, send_sem=send, recv_sem=recv,
        device_id=device, device_id_type=pl.DeviceIdType.MESH,
    )


def wrap(v, n):
    return lax.rem(v + n, n)


def inverse_factor(small):
    count = RANK // 8
    tiles = [small[8 * t:8 * t + 8] for t in range(count)]
    lane = lax.broadcasted_iota(jnp.int32, (8, 128), 1)
    sub = lax.broadcasted_iota(jnp.int32, (8, 128), 0)

    def over_lanes(v, j):
        return jnp.broadcast_to(v[:, j:j + 1], (8, 128))

    def over_rows(v, k):
        return jnp.broadcast_to(v[k:k + 1, :], (8, 128))

    out = []
    for t in range(count):
        v = tiles[t]
        cols = [over_lanes(v, 8 * t + k) for k in range(8)]
        below = [[over_lanes(tiles[r], 8 * t + k) for k in range(8)] for r in range(t + 1, count)]
        kept = jnp.zeros((8, 128), F32)
        pivots = jnp.ones((8, 128), F32)
        for k in range(8):
            at = sub == k
            here = lane == 8 * t + k
            pivot = over_rows(cols[k], k)
            inv = 1.0 / pivot
            row = jnp.where(here, 1.0, over_rows(v, k))
            kept = jnp.where(at, row, kept)
            pivots = jnp.where(at, pivot, pivots)
            scaled = row * inv
            v = jnp.where(at, scaled, jnp.where(here, 0.0, v) - cols[k] * scaled)
            for m in range(k + 1, 8):
                entry = over_rows(cols[m], k) * inv
                cols[m] = jnp.where(at, entry, cols[m] - cols[k] * entry)
        rows = [over_rows(v, k) for k in range(8)]
        block = (lane >= 8 * t) & (lane < 8 * t + 8)
        for r in range(t + 1, count):
            p = [below[r - t - 1][k] * rows[k] for k in range(8)]
            total = ((p[0] + p[1]) + (p[2] + p[3])) + ((p[4] + p[5]) + (p[6] + p[7]))
            tiles[r] = jnp.where(block, 0.0, tiles[r]) - total
        out.append(jnp.where(lane <= sub + 8 * t, kept * lax.rsqrt(pivots), 0.0))
    return jnp.concatenate(out, axis=0)


def permutation(transposed):
    p = lax.broadcasted_iota(jnp.int32, (PAD1, PAD1), 0 if transposed else 1)
    i = lax.broadcasted_iota(jnp.int32, (PAD1, PAD1), 1 if transposed else 0)
    q = p - ROW_T
    wide = ROWS * ((p & 255) >> 4) + (p & 15) + jnp.where(p >= ROW_B, 16, 0)
    narrow = ROWS * ((p - ROW_C) >> 3) + 32 + (p & 7)
    rest = ROWS * (q & 15) + 40 + (q >> 4)
    row = jnp.where(p < ROW_C, wide, jnp.where(p < ROW_T, narrow, jnp.where(p < I1, rest, p)))
    return jnp.where(row == i, 1.0, 0.0).astype(BF16)


def permuted(x, ones):
    hi = x.astype(BF16)
    left = x - hi.astype(F32)
    mid = left.astype(BF16)
    low = (left - mid.astype(F32)).astype(BF16)

    def d(u):
        return lax.dot_general(u, ones, NN, preferred_element_type=F32)

    return d(hi) + (d(mid) + d(low))


ROW_B, ROW_C, ROW_T = 256, 512, 640
BATCHES = (
    [(0, 0), (1, 0), (1, 1), (5, 0), (5, 1), (5, 5)],
    [(2, 0), (2, 1), (2, 2), (3, 0), (3, 1), (3, 2), (3, 3), (5, 2), (5, 3)],
    [(4, 0), (4, 1), (4, 2), (4, 3), (4, 4), (5, 4)],
)
SLOTS = (2, 4, 3)


def block_rows(i):
    return 32 if i == 5 else 128


def far(step, size):
    return min(step, size - step)


ALONG_Z = sorted([(dz, dc) for dz in range(NZ) for dc in range(2) if dz or dc], key=lambda o: (-far(o[0], NZ), o[1], o[0]))
ACROSS = sorted([(dx, dy) for dx in range(4) for dy in range(4) if dx or dy], key=lambda o: (-far(o[0], 4) - far(o[1], 4), o))
SEM_B, SEM_Z, SEM_E, SEM_F, SEMS = 1, 17, 25, 41, 57


def mesh_signal(sem, device):
    pl.semaphore_signal(sem, inc=1, device_id=device, device_id_type=pl.DeviceIdType.MESH)


class Sum:
    def __init__(self, batch, refs, sems, send, f, r):
        self.count = SLOTS[batch]
        self.part, self.ra, self.sa, self.rb, self.own, self.rz, self.full = refs
        self.sems = sems.at[batch]
        self.send = send
        self.r, self.z, self.c = r, f // 2, lax.rem(f, 2)
        self.other = {"fibre": self.z * 2 + (1 - self.c)}
        self.tiles = {}
        at = 0
        for i, j in BATCHES[batch]:
            self.tiles[i, j] = at
            at += block_rows(i) // 8
        for n in range(at, 2 * NR * self.count):
            self.part[self.index(n)] = jnp.zeros((8, 128), F32)

    def index(self, n):
        return n // (NR * self.count), (n // self.count) % NR, n % self.count

    def put(self, i, j, value):
        for k in range(block_rows(i) // 8):
            self.part[self.index(self.tiles[i, j] + k)] = value[8 * k:8 * k + 8]

    def get(self, i, j):
        first = self.tiles[i, j]
        return jnp.concatenate([self.full[self.index(first + k)] for k in range(block_rows(i) // 8)], axis=0)

    def copy(self, src, dst, sem, device):
        return remote(src, dst, self.sems.at[0, sem], self.sems.at[1, sem], device)

    def rest(self, offset, sign=1):
        x, y = self.r // 4, lax.rem(self.r, 4)
        return wrap(x + sign * offset[0], 4) * 4 + wrap(y + sign * offset[1], 4)

    def a(self):
        return self.copy(self.part.at[1 - self.c], self.ra, 0, self.other)

    def b(self, o):
        to = self.rest(o)
        k = 4 * o[0] + o[1]
        return self.copy(self.sa.at[to], self.rb.at[k], SEM_B + k, {"rest": to})

    def along(self, d):
        return self.copy(self.own, self.rz.at[self.z], SEM_Z + d, {"fibre": wrap(self.z + d, NZ) * 2 + self.c})

    def e(self, o):
        mine = self.full.at[self.c, self.r]
        return self.copy(mine, mine, SEM_E + 4 * o[0] + o[1], {"rest": self.rest(o)})

    def f(self, o):
        piece = self.full.at[self.c, self.rest(o, -1)]
        return self.copy(piece, piece, SEM_F + 4 * o[0] + o[1], self.other)

    def start(self):
        self.send(self.a())

    def spread(self):
        self.a().wait_recv()
        self.sa[...] = self.part[self.c] + self.ra[...]
        for o in ACROSS:
            self.send(self.b(o))

    def up(self):
        total = self.sa[self.r]
        for o in ACROSS:
            self.b(o).wait_recv()
            total = total + self.rb[4 * o[0] + o[1]]
        self.own[...] = total
        self.rz[self.z] = total
        for d in (4, 3, 5, 2, 6, 1, 7):
            self.send(self.along(d))

    def back(self):
        for d in range(1, NZ):
            self.along(d).wait_recv()
        s = [self.rz[k] for k in range(NZ)]
        self.full[self.c, self.r] = ((s[0] + s[1]) + (s[2] + s[3])) + ((s[4] + s[5]) + (s[6] + s[7]))
        for o in ACROSS:
            self.send(self.e(o))
        self.send(self.f((0, 0)))

    def finish(self):
        for o in reversed(ACROSS):
            self.e(o).wait_recv()
            self.send(self.f(o))
        for o in [(0, 0)] + ACROSS:
            self.f(o).wait_recv()


def main_kernel(slab, start, factor, core, fc, fh, fl, tail, tail_out, tail_in, gh, gl, basis, turned, core_tiles,
                s_own, s_x, r_x, s_z, r_z, s_o, s_sum, *sum_refs):
    f = lax.axis_index("fibre")
    r = lax.axis_index("rest")
    z = f // 2
    c = lax.rem(f, 2)

    sent = []

    def send(copy):
        copy.start()
        sent.append(copy)

    barrier = pltpu.get_barrier_semaphore()
    for d in range(1, NF):
        mesh_signal(barrier, {"fibre": wrap(f + d, NF)})
    for d in range(1, NR):
        mesh_signal(barrier, {"rest": wrap(r + d, NR)})

    sets = [(0, 16, 0), (16, 16, ROW_B), (32, 8, ROW_C)]

    def partner(o):
        dz, dc = o
        return wrap(z + dz, NZ) * 2 + (c if dc == 0 else 1 - c)

    def piece(k, to):
        at, rows, _ = sets[k]
        return slab.at[pl.ds(at, rows), pl.ds(pl.multiple_of(to * OWN, OWN), OWN)]

    def place(k):
        _, rows, base = sets[k]
        return fc.at[pl.ds(pl.multiple_of(base + f * rows, rows), rows), :]

    def x_copy(k, o):
        to = partner(o)
        n = 2 * o[0] + o[1]
        return remote(piece(k, to), place(k), s_x.at[k, n], r_x.at[k, n], {"fibre": to})

    def t_copy(o):
        to = partner(o)
        n = 2 * o[0] + o[1]
        return remote(tail_out.at[to], tail_in.at[f], s_x.at[3, n], r_x.at[3, n], {"fibre": to})

    tail_copy = pltpu.make_async_copy(slab.at[pl.ds(40, 2), :], tail.at[pl.ds(0, 2), :], s_own.at[3])
    tail_copy.start()
    own_copies = [pltpu.make_async_copy(piece(k, f), place(k), s_own.at[k]) for k in range(3)]
    for copy in own_copies:
        copy.start()
    pl.semaphore_wait(barrier, NF - 1 + NR - 1)

    for o in ALONG_Z:
        send(x_copy(0, o))
    tail_copy.wait()
    for to in range(NF):
        for k in range(8):
            both = tail[0:2, pl.ds((to * 8 + k) * 128, 128)]
            tail_out[to, 0, k:k + 1, :] = both[0:1]
            tail_out[to, 1, k:k + 1, :] = both[1:2]
    tail_in[f] = tail_out[f]
    for o in ALONG_Z:
        send(t_copy(o))
    for k in (1, 2):
        for o in ALONG_Z:
            send(x_copy(k, o))

    sums = [Sum(k, sum_refs[7 * k:7 * k + 7], s_sum, send, f, r) for k in range(3)]

    def rounded(top, rows):
        at = pl.ds(top, rows)
        fh[at, :], fl[at, :] = split(fc[at, :])

    def pair(top, rows):
        return fh[pl.ds(top, rows), :], fl[pl.ds(top, rows), :]

    def wait_set(k):
        own_copies[k].wait()
        for o in ALONG_Z:
            x_copy(k, o).wait_recv()

    def put(batch, i0, value, j0=0):
        step = block_rows(i0)
        for i, j in BATCHES[batch]:
            top, left = (i - i0) * step, (j - j0) * 128
            if 0 <= top < value.shape[0] and 0 <= left < value.shape[1] and (i == 5) == (i0 == 5):
                sums[batch].put(i, j, value[top:top + step, left:left + 128])

    def unpack(batch):
        for i, j in BATCHES[batch]:
            value = sums[batch].get(i, j)
            if i == 5:
                value = jnp.concatenate([value, jnp.zeros((96, 128), F32)], axis=0)
            for at, v in [((i, j), value)] + ([((j, i), value.T)] if i != j else []):
                where = (pl.ds(at[0] * 128, 128), pl.ds(at[1] * 128, 128))
                gh[where], gl[where] = split(v)

    fc[pl.ds(I1, PAD1 - I1), :] = jnp.zeros((PAD1 - I1, OWN), F32)
    wide_start = jnp.concatenate([start[...], jnp.zeros((RANK, PAD1 - I1), F32)], axis=1)
    basis[...] = permuted(wide_start, permutation(False))

    wait_set(0)
    rounded(0, 256)
    put(0, 0, dot3(pair(0, 256), pair(0, 256), NT))
    for o in ALONG_Z:
        t_copy(o).wait_recv()
    for i in range(2):
        for k in range(8):
            fc[pl.ds(ROW_T + 16 * i, 16), pl.ds(128 * k, 128)] = jnp.concatenate(
                [tail_in[s, i, k:k + 1, :] for s in range(NF)], axis=0)
    rounded(ROW_T, PAD1 - ROW_T)
    put(0, 5, dot3(pair(ROW_T, 32), pair(0, 256), NT))
    put(0, 5, dot3(pair(ROW_T, 32), pair(ROW_T, 128), NT), 5)
    sums[0].start()
    sums[0].spread()
    sums[0].up()

    wait_set(1)
    rounded(ROW_B, 256)
    put(1, 2, dot3(pair(ROW_B, 256), pair(0, 512), NT))
    put(1, 5, dot3(pair(ROW_T, 32), pair(ROW_B, 256), NT), 2)
    sums[1].start()
    sums[1].spread()
    sums[1].up()

    wait_set(2)
    rounded(ROW_C, 128)
    put(2, 4, dot3(pair(ROW_C, 128), pair(0, 640), NT))
    put(2, 5, dot3(pair(ROW_T, 32), pair(ROW_C, 128), NT), 4)
    sums[2].start()
    sums[2].spread()
    sums[0].back()
    sums[1].back()
    sums[2].up()
    sums[0].finish()
    sums[1].finish()
    unpack(0)
    unpack(1)
    sums[2].back()
    sums[2].finish()
    unpack(2)

    def step(_, carry):
        image = dot3(split(basis[...]), (gh[...], gl[...]), NN)
        wide = jnp.concatenate([image, jnp.zeros((128 - RANK, PAD1), F32)], axis=0)
        small = lax.dot_general(image, wide, NT, precision=HP, preferred_element_type=F32)
        inverse = inverse_factor(small)[:, :RANK]
        basis[...] = lax.dot_general(inverse, image, NN, precision=HP, preferred_element_type=F32)
        return carry

    lax.fori_loop(0, ITERS, step, 0)

    product = dot3(split(basis[...]), (fh[...], fl[...]), NN)
    for k in range(8):
        core_tiles[pl.ds(k, RANK, stride=8), :] = product[:, 128 * k:128 * k + 128]

    def z_copy(o):
        to = partner(o)
        n = 2 * o[0] + o[1]
        return remote(core_tiles.at[pl.ds(pl.multiple_of(to * 48, 8), 48), :],
                      core.at[pl.ds(pl.multiple_of(f * 48, 8), 48), :],
                      s_z.at[n], r_z.at[n], {"fibre": to})

    for o in ALONG_Z:
        send(z_copy(o))
    own_at = pl.ds(pl.multiple_of(f * 48, 8), 48)
    core_copy = pltpu.make_async_copy(core_tiles.at[own_at, :], core.at[own_at, :], s_o.at[0])
    core_copy.start()
    turned[...] = permuted(basis[...], permutation(True))[:, :I1]
    factor_copy = pltpu.make_async_copy(turned, factor, s_o.at[1])
    factor_copy.start()

    for o in ALONG_Z:
        z_copy(o).wait_recv()
    for copy in sent:
        copy.wait_send()
    core_copy.wait()
    factor_copy.wait()


def main_call(slab, start):
    dma = pltpu.SemaphoreType.DMA
    any_spec = pl.BlockSpec(memory_space=pl.ANY)

    def tiles(*shape):
        return pltpu.VMEM((*shape, 8, 128), F32)

    sum_scratch = []
    for n in SLOTS:
        sum_scratch += [tiles(2, NR, n), tiles(NR, n), tiles(NR, n), tiles(NR, n), tiles(n), tiles(NZ, n), tiles(2, NR, n)]
    return pl.pallas_call(
        main_kernel,
        out_shape=(
            jax.ShapeDtypeStruct((RANK, I1), F32),
            jax.ShapeDtypeStruct((RANK * 8, 128), F32),
        ),
        in_specs=[any_spec, pl.BlockSpec(memory_space=pltpu.VMEM)],
        out_specs=(any_spec, any_spec),
        scratch_shapes=[
            pltpu.VMEM((PAD1, OWN), F32),
            pltpu.VMEM((PAD1, OWN), BF16),
            pltpu.VMEM((PAD1, OWN), BF16),
            pltpu.VMEM((8, COLS), F32),
            tiles(NF, 2), tiles(NF, 2),
            pltpu.VMEM((PAD1, PAD1), BF16),
            pltpu.VMEM((PAD1, PAD1), BF16),
            pltpu.VMEM((RANK, PAD1), F32),
            pltpu.VMEM((RANK, I1), F32),
            pltpu.VMEM((RANK * 8, 128), F32),
            dma((4,)),
            dma((4, NF)), dma((4, NF)),
            dma((NF,)), dma((NF,)),
            dma((2,)),
            dma((3, 2, SEMS)),
        ] + sum_scratch,
        compiler_params=pltpu.CompilerParams(
            collective_id=0, has_side_effects=True, vmem_limit_bytes=VMEM_LIMIT),
        name="main",
    )(slab, start)


def layout_kernel(turned, tiles, factor, core):
    factor[...] = turned[...]
    for s in range(NF):
        for k in range(8):
            core[:, pl.ds((8 * s + k) * 128, 128)] = tiles[pl.ds(48 * s + k, RANK // NF, stride=8), :]


def layout_call(turned, tiles):
    vmem = pl.BlockSpec(memory_space=pltpu.VMEM)
    return pl.pallas_call(
        layout_kernel,
        out_shape=(
            jax.ShapeDtypeStruct((RANK, I1), F32),
            jax.ShapeDtypeStruct((RANK // NF, COLS), F32),
        ),
        in_specs=[vmem, vmem],
        out_specs=(vmem, vmem),
        compiler_params=pltpu.CompilerParams(vmem_limit_bytes=VMEM_LIMIT),
        name="layout",
    )(turned, tiles)


def shards(slab, start_basis):
    factor, core = layout_call(*main_call(slab, start_basis.T))
    return factor.T, core


def solution(mesh):
    return jax.shard_map(
        shards,
        mesh=mesh,
        in_specs=(P("fibre", "rest"), P()),
        out_specs=(P(), P("fibre", "rest")),
        check_vma=False,
    )
```

time: 133 us -> 129 us (0.970)
  Pallas kernels: 132 us -> 128 us
    pallas_call x1, Pallas kernels: 130 us -> 126 us  [main_call(): pl.pallas_call(main_kernel, out_shape=(jax.ShapeDtypeStruct((RANK, I1), F...]
where the time goes in v5:
time: 129 us
  Pallas kernels  128 us (99%)
    pallas_call x1, Pallas kernels, main_call(): pl.pallas_call(main_kernel, out_shape=(jax.ShapeDtypeStruct((RANK, I1), F...  126 us

profile of v5, /device:TPU:1, one launch (start us, length us, event | category | flops | bytes accessed | tf_op | source)
XLA Modules:
  0.0 128.5 jit_solution(12663026585282458583)
XLA Ops:
  0.6 125.8 %main.1 = (f32[96,672]{1,0:T(8,128)}, f32[768,128]{1,0:T(8,128)}) custom-call(f32[42,16384]{1,0:T(8,128)} %slab.1, f32[96,672]{1,0:T(8,128)} %bitcast.2), custom_call_target="tpu_custom_call" | custom-call | tf_op jit(solution)/shard_map/main/pallas_call | solution.py:422
  126.4 2.1 %layout.1 = (f32[96,672]{1,0:T(8,128)}, f32[6,16384]{1,0:T(8,128)}) custom-call(f32[96,672]{1,0:T(8,128)} %get-tuple-element.6.turned, f32[768,128]{1,0:T(8,128)} %get-tuple-element.7.tiles), custom_call_target="tpu_custom_call" | custom-call | tf_op jit(solution)/shard_map/layout/pallas_call | solution.py:462

commit v6 on v5

--- a/solution.py
+++ b/solution.py
@@ -51,8 +51,10 @@
     return lax.rem(v + n, n)
 
 
-def inverse_factor(small):
+def inverse_factor(small, beside):
     count = RANK // 8
+    width = 16
+    span = width // 8
     tiles = [small[8 * t:8 * t + 8] for t in range(count)]
     lane = lax.broadcasted_iota(jnp.int32, (8, 128), 1)
     sub = lax.broadcasted_iota(jnp.int32, (8, 128), 0)
@@ -64,32 +66,41 @@
         return jnp.broadcast_to(v[k:k + 1, :], (8, 128))
 
     out = []
-    for t in range(count):
-        v = tiles[t]
-        cols = [over_lanes(v, 8 * t + k) for k in range(8)]
-        below = [[over_lanes(tiles[r], 8 * t + k) for k in range(8)] for r in range(t + 1, count)]
-        kept = jnp.zeros((8, 128), F32)
-        pivots = jnp.ones((8, 128), F32)
-        for k in range(8):
-            at = sub == k
-            here = lane == 8 * t + k
-            pivot = over_rows(cols[k], k)
+    for t in range(0, count, span):
+        first = 8 * t
+        v = tiles[t:t + span]
+        cols = [[over_lanes(u, first + k) for u in v] for k in range(width)]
+        if t // span < len(beside):
+            beside[t // span]()
+        kept = [jnp.zeros((8, 128), F32) for _ in v]
+        pivots = [jnp.ones((8, 128), F32) for _ in v]
+        for k in range(width):
+            w, i = divmod(k, 8)
+            at = sub == i
+            here = lane == first + k
+            pivot = over_rows(cols[k][w], i)
             inv = 1.0 / pivot
-            row = jnp.where(here, 1.0, over_rows(v, k))
-            kept = jnp.where(at, row, kept)
-            pivots = jnp.where(at, pivot, pivots)
-            scaled = row * inv
-            v = jnp.where(at, scaled, jnp.where(here, 0.0, v) - cols[k] * scaled)
-            for m in range(k + 1, 8):
-                entry = over_rows(cols[m], k) * inv
-                cols[m] = jnp.where(at, entry, cols[m] - cols[k] * entry)
-        rows = [over_rows(v, k) for k in range(8)]
-        block = (lane >= 8 * t) & (lane < 8 * t + 8)
-        for r in range(t + 1, count):
-            p = [below[r - t - 1][k] * rows[k] for k in range(8)]
-            total = ((p[0] + p[1]) + (p[2] + p[3])) + ((p[4] + p[5]) + (p[6] + p[7]))
-            tiles[r] = jnp.where(block, 0.0, tiles[r]) - total
-        out.append(jnp.where(lane <= sub + 8 * t, kept * lax.rsqrt(pivots), 0.0))
+            row = jnp.where(here, 1.0, over_rows(v[w], i))
+            kept[w] = jnp.where(at, row, kept[w])
+            pivots[w] = jnp.where(at, pivot, pivots[w])
+            times = [jnp.where(at, -1.0, u) if n == w else u for n, u in enumerate(cols[k])]
+            for n in range(span):
+                clear = (here | at) if n == w else here
+                v[n] = jnp.where(clear, 0.0, v[n]) - (times[n] * row) * inv
+            for m in range(k + 1, width):
+                entry = over_rows(cols[m][w], i)
+                for n in range(span):
+                    base = jnp.where(at, 0.0, cols[m][n]) if n == w else cols[m][n]
+                    cols[m][n] = base - (times[n] * entry) * inv
+        rows = [over_rows(v[k // 8], k % 8) for k in range(width)]
+        block = (lane >= first) & (lane < first + width)
+        for r in range(t + span, count):
+            p = [over_lanes(tiles[r], first + k) * rows[k] for k in range(width)]
+            while len(p) > 1:
+                p = [p[n] + p[n + 1] for n in range(0, len(p), 2)]
+            tiles[r] = jnp.where(block, 0.0, tiles[r]) - p[0]
+        for n in range(span):
+            out.append(jnp.where(lane <= sub + 8 * (t + n), kept[n] * lax.rsqrt(pivots[n]), 0.0))
     return jnp.concatenate(out, axis=0)
 
 
@@ -135,7 +146,7 @@
 
 ALONG_Z = sorted([(dz, dc) for dz in range(NZ) for dc in range(2) if dz or dc], key=lambda o: (-far(o[0], NZ), o[1], o[0]))
 ACROSS = sorted([(dx, dy) for dx in range(4) for dy in range(4) if dx or dy], key=lambda o: (-far(o[0], 4) - far(o[1], 4), o))
-SEM_B, SEM_Z, SEM_E, SEM_F, SEMS = 1, 17, 25, 41, 57
+SEM_B, SEM_Z, SEM_E, SEM_F, SEMS = 1, 17, 25, 41, 42
 
 
 def mesh_signal(sem, device):
@@ -191,10 +202,6 @@
         mine = self.full.at[self.c, self.r]
         return self.copy(mine, mine, SEM_E + 4 * o[0] + o[1], {"rest": self.rest(o)})
 
-    def f(self, o):
-        piece = self.full.at[self.c, self.rest(o, -1)]
-        return self.copy(piece, piece, SEM_F + 4 * o[0] + o[1], self.other)
-
     def start(self):
         self.send(self.a())
 
@@ -221,17 +228,17 @@
         self.full[self.c, self.r] = ((s[0] + s[1]) + (s[2] + s[3])) + ((s[4] + s[5]) + (s[6] + s[7]))
         for o in ACROSS:
             self.send(self.e(o))
-        self.send(self.f((0, 0)))
 
     def finish(self):
-        for o in reversed(ACROSS):
+        for o in ACROSS:
             self.e(o).wait_recv()
-            self.send(self.f(o))
-        for o in [(0, 0)] + ACROSS:
-            self.f(o).wait_recv()
-
-
-def main_kernel(slab, start, factor, core, fc, fh, fl, tail, tail_out, tail_in, gh, gl, basis, turned, core_tiles,
+        half = self.full.at[self.c]
+        copy = self.copy(half, half, SEM_F, self.other)
+        self.send(copy)
+        copy.wait_recv()
+
+
+def main_kernel(slab, start, factor, core, fc, fh, fl, tail, tail_out, tail_in, gh, gl, basis, ahead, turned, core_tiles,
                 s_own, s_x, r_x, s_z, r_z, s_o, s_sum, *sum_refs):
     f = lax.axis_index("fibre")
     r = lax.axis_index("rest")
@@ -361,27 +368,44 @@
     sums[2].start()
     sums[2].spread()
     sums[0].back()
+    sums[2].up()
     sums[1].back()
-    sums[2].up()
+    sums[2].back()
     sums[0].finish()
     sums[1].finish()
     unpack(0)
     unpack(1)
-    sums[2].back()
     sums[2].finish()
     unpack(2)
 
-    def step(_, carry):
-        image = dot3(split(basis[...]), (gh[...], gl[...]), NN)
+    def exact(u, v):
+        return lax.dot_general(u, v, NN, precision=HP, preferred_element_type=F32)
+
+    def beside_factor(high, low, width):
+        image = basis[...]
+        parts = split(image)
         wide = jnp.concatenate([image, jnp.zeros((128 - RANK, PAD1), F32)], axis=0)
         small = lax.dot_general(image, wide, NT, precision=HP, preferred_element_type=F32)
-        inverse = inverse_factor(small)[:, :RANK]
-        basis[...] = lax.dot_general(inverse, image, NN, precision=HP, preferred_element_type=F32)
+
+        def piece(at):
+            def work():
+                ahead[:, at] = dot3(parts, (high[:, at], low[:, at]), NN)
+            return work
+
+        work = [piece(pl.ds(k, 256)) for k in range(0, width, 256)]
+        return inverse_factor(small, work)[:, :RANK]
+
+    basis[...] = dot3(split(basis[...]), (gh[...], gl[...]), NN)
+
+    def step(_, carry):
+        inverse = beside_factor(gh, gl, PAD1)
+        basis[...] = exact(inverse, ahead[:, pl.ds(0, PAD1)])
         return carry
 
-    lax.fori_loop(0, ITERS, step, 0)
-
-    product = dot3(split(basis[...]), (fh[...], fl[...]), NN)
+    lax.fori_loop(0, ITERS - 1, step, 0)
+    inverse = beside_factor(fh, fl, OWN)
+
+    product = exact(inverse, ahead[...])
     for k in range(8):
         core_tiles[pl.ds(k, RANK, stride=8), :] = product[:, 128 * k:128 * k + 128]
 
@@ -397,7 +421,7 @@
     own_at = pl.ds(pl.multiple_of(f * 48, 8), 48)
     core_copy = pltpu.make_async_copy(core_tiles.at[own_at, :], core.at[own_at, :], s_o.at[0])
     core_copy.start()
-    turned[...] = permuted(basis[...], permutation(True))[:, :I1]
+    turned[...] = permuted(exact(inverse, basis[...]), permutation(True))[:, :I1]
     factor_copy = pltpu.make_async_copy(turned, factor, s_o.at[1])
     factor_copy.start()
 
@@ -436,6 +460,7 @@
             pltpu.VMEM((PAD1, PAD1), BF16),
             pltpu.VMEM((PAD1, PAD1), BF16),
             pltpu.VMEM((RANK, PAD1), F32),
+            pltpu.VMEM((RANK, OWN), F32),
             pltpu.VMEM((RANK, I1), F32),
             pltpu.VMEM((RANK * 8, 128), F32),
             dma((4,)),

time: 129 us -> 124 us (0.961)
  Pallas kernels: 128 us -> 123 us
    pallas_call x1, Pallas kernels: 126 us -> 121 us  [main_call(): pl.pallas_call(main_kernel, out_shape=(jax.ShapeDtypeStruct((RANK, I1), F...]
where the time goes in v6:
time: 124 us
  Pallas kernels  123 us (99%)
    pallas_call x1, Pallas kernels, main_call(): pl.pallas_call(main_kernel, out_shape=(jax.ShapeDtypeStruct((RANK, I1), F...  121 us

profile of v6, /device:TPU:1, one launch (start us, length us, event | category | flops | bytes accessed | tf_op | source)
XLA Modules:
  0.0 123.5 jit_solution(2931378532821490066)
XLA Ops:
  0.6 120.8 %main.1 = (f32[96,672]{1,0:T(8,128)}, f32[768,128]{1,0:T(8,128)}) custom-call(f32[42,16384]{1,0:T(8,128)} %slab.1, f32[96,672]{1,0:T(8,128)} %bitcast.2), custom_call_target="tpu_custom_call" | custom-call | tf_op jit(solution)/shard_map/main/pallas_call | solution.py:446
  121.4 2.1 %layout.1 = (f32[96,672]{1,0:T(8,128)}, f32[6,16384]{1,0:T(8,128)}) custom-call(f32[96,672]{1,0:T(8,128)} %get-tuple-element.6.turned, f32[768,128]{1,0:T(8,128)} %get-tuple-element.7.tiles), custom_call_target="tpu_custom_call" | custom-call | tf_op jit(solution)/shard_map/layout/pallas_call | solution.py:487

commit v7 on v6

--- a/solution.py
+++ b/solution.py
@@ -37,7 +37,9 @@
     def d(u, v):
         return lax.dot_general(u, v, dims, preferred_element_type=F32)
 
-    return d(ah, bh) + (d(ah, bl) + d(al, bh))
+    both = d(jnp.concatenate([ah, al], axis=0), bh)
+    rows = ah.shape[0]
+    return both[:rows] + (d(ah, bl) + both[rows:])
 
 
 def remote(src, dst, send, recv, device):
@@ -129,11 +131,12 @@
 
 ROW_B, ROW_C, ROW_T = 256, 512, 640
 BATCHES = (
-    [(0, 0), (1, 0), (1, 1), (5, 0), (5, 1), (5, 5)],
-    [(2, 0), (2, 1), (2, 2), (3, 0), (3, 1), (3, 2), (3, 3), (5, 2), (5, 3)],
-    [(4, 0), (4, 1), (4, 2), (4, 3), (4, 4), (5, 4)],
+    [(0, 0), (1, 0), (1, 1)],
+    [(2, 0), (2, 1), (2, 2), (3, 0), (3, 1), (3, 2), (3, 3)],
+    [(4, 0), (4, 1), (4, 2), (4, 3), (4, 4)],
+    [(5, 0), (5, 1), (5, 2), (5, 3), (5, 4), (5, 5)],
 )
-SLOTS = (2, 4, 3)
+SLOTS = (2, 4, 3, 1)
 
 
 def block_rows(i):
@@ -276,10 +279,13 @@
         n = 2 * o[0] + o[1]
         return remote(piece(k, to), place(k), s_x.at[k, n], r_x.at[k, n], {"fibre": to})
 
+    def tail_rows(ref, at):
+        return ref.at[pl.ds(pl.multiple_of(at * 16, 16), 16), :]
+
     def t_copy(o):
         to = partner(o)
         n = 2 * o[0] + o[1]
-        return remote(tail_out.at[to], tail_in.at[f], s_x.at[3, n], r_x.at[3, n], {"fibre": to})
+        return remote(tail_rows(tail_out, to), tail_rows(tail_in, f), s_x.at[3, n], r_x.at[3, n], {"fibre": to})
 
     tail_copy = pltpu.make_async_copy(slab.at[pl.ds(40, 2), :], tail.at[pl.ds(0, 2), :], s_own.at[3])
     tail_copy.start()
@@ -290,20 +296,18 @@
 
     for o in ALONG_Z:
         send(x_copy(0, o))
+    for k in (1, 2):
+        for o in ALONG_Z:
+            send(x_copy(k, o))
     tail_copy.wait()
     for to in range(NF):
         for k in range(8):
-            both = tail[0:2, pl.ds((to * 8 + k) * 128, 128)]
-            tail_out[to, 0, k:k + 1, :] = both[0:1]
-            tail_out[to, 1, k:k + 1, :] = both[1:2]
-    tail_in[f] = tail_out[f]
+            tail_out[pl.ds(to * 16 + k, 2, stride=8), :] = tail[0:2, pl.ds((to * 8 + k) * 128, 128)]
+    tail_rows(tail_in, f)[...] = tail_rows(tail_out, f)[...]
     for o in ALONG_Z:
         send(t_copy(o))
-    for k in (1, 2):
-        for o in ALONG_Z:
-            send(x_copy(k, o))
-
-    sums = [Sum(k, sum_refs[7 * k:7 * k + 7], s_sum, send, f, r) for k in range(3)]
+
+    sums = [Sum(k, sum_refs[7 * k:7 * k + 7], s_sum, send, f, r) for k in range(4)]
 
     def rounded(top, rows):
         at = pl.ds(top, rows)
@@ -340,43 +344,46 @@
     wait_set(0)
     rounded(0, 256)
     put(0, 0, dot3(pair(0, 256), pair(0, 256), NT))
+    sums[0].start()
+    sums[0].spread()
+    sums[0].up()
+
+    wait_set(1)
+    rounded(ROW_B, 256)
+    put(1, 2, dot3(pair(ROW_B, 256), pair(0, 512), NT))
+    sums[1].start()
+    sums[1].spread()
+    sums[1].up()
+
+    wait_set(2)
+    rounded(ROW_C, 128)
+    put(2, 4, dot3(pair(ROW_C, 128), pair(0, 640), NT))
+    sums[2].start()
+    sums[2].spread()
+
     for o in ALONG_Z:
         t_copy(o).wait_recv()
     for i in range(2):
         for k in range(8):
-            fc[pl.ds(ROW_T + 16 * i, 16), pl.ds(128 * k, 128)] = jnp.concatenate(
-                [tail_in[s, i, k:k + 1, :] for s in range(NF)], axis=0)
+            fc[pl.ds(ROW_T + 16 * i, 16), pl.ds(128 * k, 128)] = tail_in[pl.ds(8 * i + k, 16, stride=16), :]
     rounded(ROW_T, PAD1 - ROW_T)
-    put(0, 5, dot3(pair(ROW_T, 32), pair(0, 256), NT))
-    put(0, 5, dot3(pair(ROW_T, 32), pair(ROW_T, 128), NT), 5)
-    sums[0].start()
-    sums[0].spread()
-    sums[0].up()
-
-    wait_set(1)
-    rounded(ROW_B, 256)
-    put(1, 2, dot3(pair(ROW_B, 256), pair(0, 512), NT))
-    put(1, 5, dot3(pair(ROW_T, 32), pair(ROW_B, 256), NT), 2)
-    sums[1].start()
-    sums[1].spread()
-    sums[1].up()
-
-    wait_set(2)
-    rounded(ROW_C, 128)
-    put(2, 4, dot3(pair(ROW_C, 128), pair(0, 640), NT))
-    put(2, 5, dot3(pair(ROW_T, 32), pair(ROW_C, 128), NT), 4)
-    sums[2].start()
-    sums[2].spread()
+    put(3, 5, dot3(pair(ROW_T, 32), pair(0, PAD1), NT))
+    sums[3].start()
+    sums[3].spread()
     sums[0].back()
     sums[2].up()
     sums[1].back()
+    sums[3].up()
     sums[2].back()
+    sums[3].back()
     sums[0].finish()
     sums[1].finish()
     unpack(0)
     unpack(1)
     sums[2].finish()
     unpack(2)
+    sums[3].finish()
+    unpack(3)
 
     def exact(u, v):
         return lax.dot_general(u, v, NN, precision=HP, preferred_element_type=F32)
@@ -456,7 +463,8 @@
             pltpu.VMEM((PAD1, OWN), BF16),
             pltpu.VMEM((PAD1, OWN), BF16),
             pltpu.VMEM((8, COLS), F32),
-            tiles(NF, 2), tiles(NF, 2),
+            pltpu.VMEM((NF * 16, 128), F32),
+            pltpu.VMEM((NF * 16, 128), F32),
             pltpu.VMEM((PAD1, PAD1), BF16),
             pltpu.VMEM((PAD1, PAD1), BF16),
             pltpu.VMEM((RANK, PAD1), F32),
@@ -467,7 +475,7 @@
             dma((4, NF)), dma((4, NF)),
             dma((NF,)), dma((NF,)),
             dma((2,)),
-            dma((3, 2, SEMS)),
+            dma((4, 2, SEMS)),
         ] + sum_scratch,
         compiler_params=pltpu.CompilerParams(
             collective_id=0, has_side_effects=True, vmem_limit_bytes=VMEM_LIMIT),

time: 124 us -> 123 us (level)
  no operation moved by 1% of the time
where the time goes in v7:
time: 123 us
  Pallas kernels  122 us (99%)
    pallas_call x1, Pallas kernels, main_call(): pl.pallas_call(main_kernel, out_shape=(jax.ShapeDtypeStruct((RANK, I1), F...  120 us

profile of v7, /device:TPU:1, one launch (start us, length us, event | category | flops | bytes accessed | tf_op | source)
XLA Modules:
  0.0 122.7 jit_solution(15366366831088832342)
XLA Ops:
  0.6 119.9 %main.1 = (f32[96,672]{1,0:T(8,128)}, f32[768,128]{1,0:T(8,128)}) custom-call(f32[42,16384]{1,0:T(8,128)} %slab.1, f32[96,672]{1,0:T(8,128)} %bitcast.2), custom_call_target="tpu_custom_call" | custom-call | tf_op jit(solution)/shard_map/main/pallas_call | solution.py:453
  120.6 2.1 %layout.1 = (f32[96,672]{1,0:T(8,128)}, f32[6,16384]{1,0:T(8,128)}) custom-call(f32[96,672]{1,0:T(8,128)} %get-tuple-element.6.turned, f32[768,128]{1,0:T(8,128)} %get-tuple-element.7.tiles), custom_call_target="tpu_custom_call" | custom-call | tf_op jit(solution)/shard_map/layout/pallas_call | solution.py:495
